TPU v7x, 32 devices: a whole 2x2x4 slice. The times are simulated.
32 devices in a mesh: seq: 16 (over z, y, x), eig: 2 (over core).
Axes of the slice: x: 2, y: 2, z: 4, core: 2. Of those that a mesh axis runs over, the one named last changes fastest.
Arguments:
- train_in: bfloat16 [2048, 5120], P('seq'), may hold values from -6 to 6
- train_out: bfloat16 [2048, 13824], P('seq'), may hold values from -6 to 6
- query_in: bfloat16 [16, 5120], P('seq'), may hold values from -6 to 6
- query_out: bfloat16 [16, 13824], P('seq'), may hold values from -6 to 6
- input_basis: bfloat16 [5120, 5120], P('seq', 'eig'), may hold values from -0.078125 to 0.078125
- output_basis: bfloat16 [13824, 6912], P('seq', 'eig'), may hold values from -0.0546875 to 0.0546875
- corrected: bfloat16 [5120, 6912], P('seq', 'eig'), may hold values from 0.0099487305 to 10
- train_seq: int32 [2048], P('seq'), may hold values from 0 to 1
- query_order: int32 [16], P('seq'), may hold values from 0 to 15, each once
Outputs:
- scores: float32 [32, 16], P('seq')
Inputs may be any that keep to these rules, and one draw needn't show every extreme that they name: query_order holds every number of 0 to 15 once, so each query has 1 token.
All inputs are finite; a program needn't handle non-finite values.
Results may differ from a plain program's by a relative error of at most 0.025.
Values may be sent and summed in bfloat16 or wider, within the bound.
No kernel may reach another device: no remote copies, remote signals or barrier semaphores. Data moves between devices by JAX's collectives and lax.ppermute only.
A program may use at most 192 MiB of HBM per device.

v0:
```python
import functools
import math

import jax
import jax.numpy as jnp
from jax import lax
from jax.experimental import pallas as pl
from jax.experimental.pallas import tpu as pltpu
from jax.sharding import PartitionSpec as P

DIN = 5120
EIGOUT = 6912
TOK_DEV = 128
SEQ_DEV = 2
QUERIES = 16
DAMPING = 0.1
INNER = 4
F32 = jnp.float32
BF16 = jnp.bfloat16
NT = (((1,), (1,)), ((), ()))
VMEM = pl.BlockSpec(memory_space=pltpu.VMEM)
SMEM = pl.BlockSpec(memory_space=pltpu.SMEM)


def bits(count):
    return range(count.bit_length() - 1)


def pick(x, index, axis=0):
    return lax.dynamic_index_in_dim(x, index, axis, keepdims=False)


def swap(x, axis, mask):
    size = lax.axis_size(axis)
    return lax.ppermute(x, axis, [(i, i ^ mask) for i in range(size)])


def unxor(x, index):
    size = x.shape[0]
    for b in bits(size):
        pairs = x.reshape((size >> (b + 1), 2, 1 << b) + x.shape[1:])
        turned = jnp.concatenate([pairs[:, 1:], pairs[:, :1]], axis=1)
        x = jnp.where((index >> b) & 1 == 1, turned, pairs).reshape(x.shape)
    return x


def after(x, *done):
    return lax.optimization_barrier((x,) + done)[0]


def add(*terms):
    total = terms[0].astype(F32)
    for term in terms[1:]:
        total = total + term.astype(F32)
    return total.astype(BF16)


EXTRA = 8


def padded(width):
    return -(-width // 128) * 128


def call(kernel, outs, *args, scratch=(), mib=40, flops=0):
    moved = sum(x.size * x.dtype.itemsize for x in list(args) + list(outs))
    return pl.pallas_call(
        kernel,
        out_shape=list(outs),
        in_specs=[SMEM] + [VMEM] * (len(args) - 1),
        out_specs=[VMEM] * len(outs),
        scratch_shapes=list(scratch),
        compiler_params=pltpu.CompilerParams(vmem_limit_bytes=mib << 20),
        cost_estimate=pl.CostEstimate(flops=flops, bytes_accessed=moved, transcendentals=0),
    )(*args)


def pack_kernel(widths, where, t_out, t_in, q_out, q_in, info, *outs):
    z, e = where[0] // INNER, where[1]
    share = outs[0].shape[0] - EXTRA
    rows = pl.ds(pl.multiple_of(e * share, 16), share)
    wide, narrow = widths
    for v in range(len(outs)):

        @pl.when(z == v)
        def _(v=v):
            for m, out in enumerate(outs):
                place = m ^ v
                for tokens, queries, width, at, last in (
                    (t_out, q_out, wide, 0, None),
                    (t_in, q_in, narrow, padded(wide), info),
                ):
                    cols = slice(place * width, (place + 1) * width)
                    out[:share, at : at + width] = tokens[rows, cols]
                    row = lax.broadcasted_iota(jnp.int32, (EXTRA, width), 0)
                    extra = jnp.zeros((EXTRA, width), F32)
                    count = queries.shape[0]
                    for i in range(count):
                        extra = jnp.where(row == i, queries[i : i + 1, cols].astype(F32), extra)
                    if last is not None:
                        extra = jnp.where(row == count, last[:, :width].astype(F32), extra)
                    out[share:, at : at + width] = extra.astype(BF16)


def pack(where, t_out, t_in, q_out, q_in, info, share, outer):
    wide, narrow = t_out.shape[1] // outer, t_in.shape[1] // outer
    shape = jax.ShapeDtypeStruct((share + EXTRA, padded(wide) + padded(narrow)), BF16)
    return call(
        functools.partial(pack_kernel, (wide, narrow)),
        [shape] * outer,
        where,
        t_out,
        t_in,
        q_out,
        q_in,
        info,
    )


def split_kernel(pieces, common, count, where, *refs):
    sources, outs = refs[:count], refs[count : count + len(pieces)]
    xy = where[0] % INNER
    if common:
        for s, source in enumerate(sources):
            refs[-1][s] = source[:, common[0] : common[1]]
    for v in range(INNER):

        @pl.when(xy == v)
        def _(v=v):
            for r, out in enumerate(outs):
                for start, stop, at in pieces[r ^ v]:
                    for s, source in enumerate(sources):
                        out[s, :, at : at + stop - start] = source[:, start:stop]


def split(where, sources, pieces, common=None):
    rows = sources[0].shape[0]
    width = max(at + stop - start for start, stop, at in pieces[0])
    outs = [jax.ShapeDtypeStruct((len(sources), rows, width), BF16)] * len(pieces)
    if common:
        outs.append(
            jax.ShapeDtypeStruct((len(sources), rows, common[1] - common[0]), BF16)
        )
    return call(
        functools.partial(split_kernel, pieces, common, len(sources)), outs, where, *sources
    )


def invert_kernel(where, *refs):
    sources, out = refs[:-1], refs[-1]
    rows = sources[0].shape[1]
    xy = where[0] % INNER
    for v in range(INNER):

        @pl.when(xy == v)
        def _(v=v):
            for r, source in enumerate(sources):
                damped = source[0].astype(F32) + DAMPING
                out[:, (r ^ v) * rows : ((r ^ v) + 1) * rows] = (1.0 / damped).T


def invert(where, sources):
    _, rows, cols = sources[0].shape
    shape = jax.ShapeDtypeStruct((cols, len(sources) * rows), F32)
    return call(invert_kernel, [shape], where, *sources)[0]


def gather_rows(parts, e, index, share, cols):
    shares = []
    for h in range(len(parts)):
        rows = parts[0][index, :share, cols]
        for m in range(1, len(parts)):
            rows = jnp.where((e ^ m) == h, parts[m][index, :share, cols], rows)
        shares.append(rows)
    return jnp.concatenate(shares, axis=0) if len(shares) > 1 else shares[0]


def grouped(refs):
    return [refs[i : i + INNER] for i in range(0, len(refs), INNER)]


def rotate_in_kernel(n, blocks, query_rows, at, where, *refs):
    pieces, refs = refs[:INNER], refs[INNER:]
    parts = refs[:-5]
    out, info, basis, rows, queries = refs[-5:]
    xy, z, e = where[0] % INNER, where[0] // INNER, where[1]
    depth = rows.shape[1]
    cols = slice(at, at + depth)
    width = basis.shape[0] // blocks
    share = TOK_DEV // len(parts)

    def store(group, product, lane):
        for k in range(blocks):
            out[k, group] = product[
                k * width : (k + 1) * width, lane * TOK_DEV : (lane + 1) * TOK_DEV
            ].astype(BF16)

    queries[...] = jnp.zeros_like(queries)
    for v in range(INNER):

        @pl.when(xy == v)
        def _(v=v):
            step = depth // INNER
            for r, piece in enumerate(pieces):
                place = (r ^ v) * step
                basis[:, place : place + step] = piece[0].astype(F32).T.astype(BF16)
            for g in range(n):
                place = ((g % INNER) ^ v) * (n // INNER) + ((g // INNER) ^ z)
                extra = parts[0][place, share:, cols].astype(F32)
                queries[g * query_rows : (g + 1) * query_rows] = extra[:query_rows]
                info[g] = extra[:, : info.shape[2]]

    store(
        n,
        lax.dot_general(
            basis[...], queries[...].astype(BF16), NT, preferred_element_type=F32
        ),
        0,
    )

    @pl.loop(0, n // INNER)
    def _(plane):
        for v in range(INNER):

            @pl.when(xy == v)
            def _(v=v):
                for p in range(INNER):
                    rows[p * TOK_DEV : (p + 1) * TOK_DEV] = gather_rows(
                        parts, e, (p ^ v) * (n // INNER) + (plane ^ z), share, cols
                    )

        product = lax.dot_general(basis[...], rows[...], NT, preferred_element_type=F32)
        for p in range(INNER):
            store(plane * INNER + p, product, p)


def rotate_in(where, pieces, parts, n, blocks, query_rows, at):
    _, width, cols = pieces[0].shape
    depth = INNER * width
    return call(
        functools.partial(rotate_in_kernel, n, blocks, query_rows, at),
        [
            jax.ShapeDtypeStruct((blocks, n + 1, cols // blocks, TOK_DEV), BF16),
            jax.ShapeDtypeStruct((n, EXTRA, 256), F32),
        ],
        where,
        *pieces,
        *parts,
        scratch=[
            pltpu.VMEM((cols, depth), BF16),
            pltpu.VMEM((INNER * TOK_DEV, depth), BF16),
            pltpu.VMEM((TOK_DEV, depth), F32),
        ],
        mib=48,
        flops=2 * (n + 1) * TOK_DEV * cols * depth,
    )


def rotate_out_kernel(chunk, outer, query_rows, where, basis, *refs):
    parts, outs = grouped(refs[:-6]), refs[-6:-2]
    rows, queries = refs[-2:]
    sx, kx, sy, ky = outs
    xy, z, e = where[0] % INNER, where[0] // INNER, where[1]
    half = outer // 2
    cols, depth = basis.shape[1], basis.shape[2]
    share = TOK_DEV // len(parts)
    total = queries.shape[0]

    for v in range(INNER):

        @pl.when((pl.program_id(0) == 0) & (xy == v))
        def _(v=v):
            for p in range(outer):
                group = chunk * outer + p
                rows[p * TOK_DEV : (p + 1) * TOK_DEV] = gather_rows(
                    [part[(p % INNER) ^ v] for part in parts],
                    e,
                    (group // INNER) ^ z,
                    share,
                    slice(0, depth),
                )
            if chunk == 0:
                for g in range(outer * INNER):
                    part = parts[0][(g % INNER) ^ v]
                    extra = part[(g // INNER) ^ z, share:, :depth].astype(F32)
                    queries[g * query_rows : (g + 1) * query_rows] = extra[:query_rows]

    product = lax.dot_general(basis[0], rows[...], NT, preferred_element_type=F32)

    def put(ref, place, first):
        for p in range(half):
            lane = (first + p) * TOK_DEV
            ref[place, p * cols : (p + 1) * cols] = product[:, lane : lane + TOK_DEV].astype(
                BF16
            )

    for r, (a, i, b, j) in enumerate(
        [(kx, 0, ky, 0), (sx, 0, ky, 1), (kx, 1, sy, 0), (sx, 1, sy, 1)]
    ):

        @pl.when(pl.program_id(0) == r)
        def _(a=a, i=i, b=b, j=j):
            put(a, i, 0)
            put(b, j, half)
            if chunk == 0:
                turned = lax.dot_general(
                    queries[...].astype(BF16), basis[0], NT, preferred_element_type=F32
                )
                rest = padded(cols) - cols
                if rest:
                    turned = jnp.concatenate([turned, jnp.zeros((total, rest), F32)], axis=1)
                for k in range(padded(cols) // 128):
                    start = half * cols + k * total
                    a[i, start : start + total] = turned[:, k * 128 : (k + 1) * 128].astype(
                        BF16
                    )


def rotate_out(where, *, basis, parts, chunk, outer, query_rows):
    _, cols, depth = basis.shape
    half = outer // 2
    total = outer * INNER * query_rows
    flat = [part for group in parts for part in group]
    extra = total * padded(cols) // 128 if chunk == 0 else 0
    first = jax.ShapeDtypeStruct((2, half * cols + extra, TOK_DEV), BF16)
    second = jax.ShapeDtypeStruct((2, half * cols, TOK_DEV), BF16)
    outs = [first, first, second, second]
    return pl.pallas_call(
        functools.partial(rotate_out_kernel, chunk, outer, query_rows),
        out_shape=outs,
        grid_spec=pltpu.PrefetchScalarGridSpec(
            num_scalar_prefetch=1,
            grid=(INNER,),
            in_specs=[pl.BlockSpec((1, cols, depth), lambda r, w: (r ^ (w[0] % INNER), 0, 0))]
            + [pl.BlockSpec(part.shape, lambda r, w: (0, 0, 0)) for part in flat],
            out_specs=[pl.BlockSpec(out.shape, lambda r, w: (0, 0, 0)) for out in outs],
            scratch_shapes=[
                pltpu.VMEM((outer * TOK_DEV, depth), BF16),
                pltpu.VMEM((total, depth), F32),
            ],
        ),
        compiler_params=pltpu.CompilerParams(vmem_limit_bytes=48 << 20),
        cost_estimate=pl.CostEstimate(
            flops=2 * outer * TOK_DEV * basis.size,
            bytes_accessed=2 * (basis.size + outer * TOK_DEV * (INNER * cols + depth)),
            transcendentals=0,
        ),
    )(where, basis, *flat)


def score_kernel(chunk, outer, masks, shares, info_row, where, b_ref, inverse, query_b, info, *refs):
    a_refs, q_refs, out, a_all = refs[:shares], refs[shares:-2], refs[-2], refs[-1]
    z, e = where[0] // INNER, where[1]
    rows, width = a_all.shape[1], a_refs[0].shape[2]
    tile = 256 if rows % 256 == 0 else 128

    def gather(sources, group, slot):
        for r in range(INNER):
            for h in range(shares):
                a = sources[0][r, group]
                for m in range(1, shares):
                    a = jnp.where((e ^ m) == h, sources[m][r, group], a)
                start = (r * shares + h) * width
                a_all[slot, start : start + width] = a

    gather(q_refs, 0, len(masks))
    for p, mask in enumerate(masks):
        place = z ^ mask
        gather(a_refs, place, p)
        seq = info[chunk * outer + place][info_row : info_row + 1, :TOK_DEV]
        for member in range(SEQ_DEV):
            b = jnp.where(seq == member, b_ref[p].astype(F32), 0.0).astype(BF16)
            total = jnp.zeros((b.shape[0], TOK_DEV), F32)
            for start in range(0, rows, tile):
                grad = lax.dot_general(
                    b, a_all[p, start : start + tile], NT, preferred_element_type=F32
                )
                scaled = (grad * inverse[:, start : start + tile]).astype(BF16)
                total = total + jnp.dot(
                    scaled,
                    a_all[len(masks), start : start + tile],
                    preferred_element_type=F32,
                )
            out[p, member : member + 1] = jnp.sum(total * query_b[...], axis=0, keepdims=True)


def score(where, b, a_parts, inverse, query_b, info, chunk, outer, masks, info_row):
    cols, rows = inverse.shape
    count = len(masks)
    _, groups, width, _ = a_parts[0].shape
    return pl.pallas_call(
        functools.partial(score_kernel, chunk, outer, masks, len(a_parts), info_row),
        out_shape=jax.ShapeDtypeStruct((count, SEQ_DEV, TOK_DEV), F32),
        grid=(1,),
        in_specs=[SMEM]
        + [VMEM] * 4
        + [pl.BlockSpec((INNER, outer, width, TOK_DEV), lambda i: (0, chunk, 0, 0))]
        * len(a_parts)
        + [pl.BlockSpec((INNER, 1, width, TOK_DEV), lambda i: (0, groups - 1, 0, 0))]
        * len(a_parts),
        out_specs=VMEM,
        scratch_shapes=[pltpu.VMEM((count + 1, rows, TOK_DEV), BF16)],
        compiler_params=pltpu.CompilerParams(vmem_limit_bytes=48 << 20),
        cost_estimate=pl.CostEstimate(
            flops=16 * count * SEQ_DEV * TOK_DEV * cols * rows,
            bytes_accessed=2 * (b.size + a_parts[0].size + 2 * inverse.size),
            transcendentals=0,
        ),
    )(where, b, inverse, query_b, info, *a_parts, *a_parts)


def body(
    train_in,
    train_out,
    query_in,
    query_out,
    input_basis,
    output_basis,
    corrected,
    train_seq,
    query_order,
):
    n, size = lax.axis_size("seq"), lax.axis_size("eig")
    outer = n // INNER
    me, e = lax.axis_index("seq"), lax.axis_index("eig")
    xy, z = me % INNER, me // INNER
    where = jnp.stack([me, e]).astype(jnp.int32)
    share = TOK_DEV // size
    query_rows = query_in.shape[0]
    queries = n * query_rows
    depth_out, cols = output_basis.shape
    cols_own = cols // INNER
    rows_own = corrected.shape[0]
    rows_in = rows_own * INNER
    per_core = input_basis.shape[1] // rows_in

    def in_plane(pieces):
        return [pieces[0]] + [swap(pieces[r], "seq", r) for r in range(1, INNER)]

    def in_turn(pieces, first, last):
        done = [swap(after(pieces[r], *first), "seq", r) for r in range(1, INNER - 1)]
        x = after(pieces[-1], *last, done[0])
        return [pieces[0]] + done + [swap(x, "seq", INNER - 1)]

    info = jnp.concatenate([train_seq, query_order % QUERIES]).astype(BF16)
    info = jnp.pad(info, (0, padded(rows_in) - info.shape[0]))[None]
    sent = pack(where, train_out, train_in, query_out, query_in, info, share, outer)
    sent = [sent[0]] + [swap(sent[m], "seq", m * INNER) for m in range(1, outer)]

    basis_pieces = in_turn(
        split(
            where,
            [after(input_basis, sent[0])],
            [
                [
                    (
                        (k * INNER + a) * rows_own,
                        (k * INNER + a + 1) * rows_own,
                        k * rows_own,
                    )
                    for k in range(per_core)
                ]
                for a in range(INNER)
            ],
        ),
        sent[1:2],
        sent[2:],
    )

    inverse = invert(
        where,
        in_turn(
            split(
                where,
                [after(corrected, sent[0])],
                [[(a * cols_own, (a + 1) * cols_own, 0)] for a in range(INNER)],
            ),
            (),
            (),
        ),
    )

    wide = padded(INNER * depth_out)
    basis_out = output_basis.reshape(depth_out, INNER, cols_own).transpose(1, 2, 0)
    *out_pieces, in_piece = split(
        after(where, inverse, basis_out, *basis_pieces[1:-1]),
        sent,
        [[(a * depth_out, (a + 1) * depth_out, 0)] for a in range(INNER)],
        (wide, wide + rows_in),
    )

    out_pieces = in_plane(out_pieces)
    parts = [out_pieces] + [
        [swap(x, "eig", m) for x in out_pieces] for m in range(1, size)
    ]
    in_rel = in_plane([after(in_piece, *out_pieces[1:], basis_pieces[-1])] * INNER)
    rotate = functools.partial(
        rotate_out, basis=basis_out, parts=parts, outer=outer, query_rows=query_rows
    )

    def plane_sum(sx, kx, sy, ky):
        rx, ry = yield (sx, 1), (sy, 2)
        low, high = yield (add(kx[1], rx[1]), 2), (add(ky[1], ry[1]), 1)
        return add(kx[0], rx[0], low), add(ky[0], ry[0], high)

    def planes_sum(held, extra=None):
        for b in bits(outer):
            bit = (z >> b) & 1
            pairs = held.reshape((-1, 2) + held.shape[1:])
            x = pick(pairs, 1 - bit, 1)
            if extra is not None:
                x = jnp.concatenate([x.reshape(-1, TOK_DEV), extra])
            (got,) = yield ((x, INNER << b),)
            if extra is not None:
                at = got.shape[0] - extra.shape[0]
                extra = add(extra, got[at:])
                got = got[:at].reshape((-1,) + held.shape[1:])
            held = add(pick(pairs, bit, 1), got)
        masks = [0]
        for b in reversed(bits(outer)):
            shape = held.shape
            flat = held.reshape(-1, TOK_DEV)
            items = [flat] if b else [flat[:16], flat[16:]]
            got = yield tuple((x, INNER << b) for x in items)
            more = [m | (1 << b) for m in masks]
            held, masks = jnp.concatenate([flat] + got), masks + more
            held = held.reshape((2 * shape[0],) + shape[1:])
        return held, masks, extra

    partial_sums = [rotate(where, chunk=0)]
    partial_sums.append(rotate(after(where, partial_sums[0][2]), chunk=1))
    in_rel = jnp.concatenate([after(x, partial_sums[0][2]) for x in in_rel])
    in_parts = [in_rel] + [swap(in_rel, "eig", m) for m in range(1, size)]
    rotated, info = rotate_in(
        after(where, partial_sums[1][2]), basis_pieces, in_parts, n, per_core, query_rows, 0
    )
    rotated = rotated.reshape(per_core, n + 1, size, rows_own // size, TOK_DEV)
    swapped = [swap(pick(rotated, e ^ m, 2), "eig", m) for m in range(1, size)]
    rotated = jnp.stack([pick(rotated, e, 2)] + swapped)
    rotated = unxor(rotated, e).reshape((outer,) + rotated.shape[2:])
    across = [[INNER * i + a for i in range(outer)] for a in range(INNER)]
    inside = [[INNER * i + a for a in range(INNER)] for i in range(outer)]
    rotated = lax.psum_scatter(
        rotated, "seq", scatter_dimension=0, tiled=True, axis_index_groups=across
    )

    def between_cores(x):
        a_parts = [x] + [swap(x, "eig", m) for m in range(1, size)]
        if a_parts[0].shape[2] % 16:
            whole = unxor(jnp.stack(a_parts), e).transpose(1, 2, 0, 3, 4)
            a_parts = [whole.reshape(INNER, n + 1, rows_own, TOK_DEV)]
        return a_parts

    active = {("plane", 0): plane_sum(*partial_sums[0])}
    got, fence, found, scored = {}, [], {}, {}
    step, query_b = 0, None
    while active:
        sends = {}
        for key in list(active):
            try:
                sends[key] = active[key].send(got.get(key))
                continue
            except StopIteration as stop:
                value = stop.value
            kind, chunk = key
            del active[key]
            if kind == "plane":
                low, high = value
                at = outer // 2 * cols_own
                held = jnp.concatenate([low[:at], high]).reshape(outer, cols_own, TOK_DEV)
                active["planes", chunk] = planes_sum(held, None if chunk else low[at:])
                sends["planes", chunk] = active["planes", chunk].send(None)
            else:
                found[chunk] = value[:2]
                if chunk == 0:
                    value = value[2].reshape(-1, queries, TOK_DEV).transpose(0, 2, 1)
                    value = value.reshape(-1, queries)[:cols_own].astype(F32)
                    query_b = jnp.pad(value, ((0, 0), (0, TOK_DEV - queries)))
        if 0 < step < INNER:
            begun = plane_sum(*partial_sums[step])
            active["plane", step] = begun
            sends["plane", step] = begun.send(None)
        if step == 2:
            fence = fence + swapped
        if step == INNER:
            gathered = lax.all_gather(
                after(rotated, *fence), "seq", axis=0, tiled=True, axis_index_groups=inside
            )
        if step == INNER + 2:
            a_parts = between_cores(after(gathered, *fence))
            fence = fence + list(a_parts)
        if 0 < step < INNER:
            fence = fence + [partial_sums[step][2]]
        got = {}
        for key, items in sends.items():
            got[key] = [swap(after(x, *fence), "seq", mask) for x, mask in items]
        if 0 < step < INNER - 1:
            partial_sums.append(rotate(after(where, *fence), chunk=step + 1))
        fence = [x for items in got.values() for x in items]
        for chunk in sorted(set(found) - set(scored)):
            held, masks = found[chunk]
            here = where
            if len(fence) > 1:
                here = after(where, min(fence, key=lambda x: x.size))
            values = score(
                here, held, a_parts, inverse, query_b, info, chunk, outer, masks, query_rows
            )
            if chunk == 0:
                fence = fence + [values]
            values = values[:, :, :queries]
            scored[chunk] = unxor(
                jnp.stack([values[masks.index(m)] for m in range(outer)]), z
            )
        step += 1
    labels = info[:, query_rows, TOK_DEV : TOK_DEV + query_rows].reshape(-1)
    hot = (labels[:, None] == jnp.arange(QUERIES, dtype=F32)[None, :]).astype(F32)
    per_token = jnp.concatenate([scored[chunk] for chunk in range(INNER)])
    scores = jnp.sum(per_token[:, :, :, None] * hot[None, None], axis=2)
    scores = lax.all_to_all(scores, "seq", split_axis=0, concat_axis=0, tiled=True)
    scores = jnp.sum(scores, axis=0)
    for b in bits(size):
        scores = scores + swap(scores, "eig", 1 << b)
    factor = 1.0 / math.sqrt(DIN * EIGOUT * (TOK_DEV / SEQ_DEV) * (queries / QUERIES))
    return scores * factor


def solution(mesh):
    placed = (
        P("seq", None),
        P("seq", None),
        P("seq", None),
        P("seq", None),
        P("seq", "eig"),
        P("seq", "eig"),
        P("seq", "eig"),
        P("seq"),
        P("seq"),
    )
    return jax.shard_map(
        body, mesh=mesh, in_specs=placed, out_specs=P("seq", None), check_vma=False
    )
```

profile of v0, /device:TPU:0, one launch (start us, length us, event | category | flops | bytes accessed | tf_op | source)
XLA Modules:
  0.0 458.6 jit_solution(13938793741932810903)
XLA Ops:
  8.0 2.0 copy-done.1
  12.8 1.9 shard_map.91
  14.7 1.9 shard_map.92
  16.7 2.9 collective-permute-start
  22.7 2.6 collective-permute-start.6
  25.5 7.1 %collective-permute-done.refs_1_ = bf16[1,320,864]{2,1,0:T(8,128)(2,1)S(1)} collective-permute-done((bf16[1,320,864]{2,1,0:T(8,128)(2,1)S(1)}, bf16[1,320,864]{2,1,0:T(8,128)(2,1)S(1)}, u32[]{:S(2)}, u32[]{:S(2)}) %collective-permute-start) | collective-permute-done | bytes 552992 | tf_op jit(solution)/shard_map/ppermute | solution.py:35
  33.4 2.7 collective-permute-start.2
  36.1 1.9 shard_map.94
  39.5 9.7 %collective-permute-done.3.refs_1_ = bf16[72,4736]{1,0:T(8,128)(2,1)S(1)} collective-permute-done((bf16[72,4736]{1,0:T(8,128)(2,1)S(1)}, bf16[72,4736]{1,0:T(8,128)(2,1)S(1)}, u32[]{:S(2)}, u32[]{:S(2)}) %collective-permute-start.3) | collective-permute-done | bytes 682016 | tf_op jit(solution)/shard_map/ppermute | solution.py:35
  49.2 2.0 collective-permute-start.5
  52.6 9.1 %copy.64 = bf16[864,3456]{0,1:T(8,128)(2,1)} copy(bf16[864,3456]{1,0:T(8,128)(2,1)} %param.14) | data formatting | bytes 11943936 | tf_op args[5]
  63.9 3.5 shard_map.93.inverse
  67.4 2.1 copy-done
  69.5 1.8 collective-permute-done.6.refs_2_
  73.5 2.5 collective-permute-start.10
  76.0 11.2 %collective-permute-done.8.refs_1_ = bf16[4,72,864]{2,1,0:T(8,128)(2,1)S(1)} collective-permute-done((bf16[4,72,864]{2,1,0:T(8,128)(2,1)S(1)}, bf16[4,72,864]{2,1,0:T(8,128)(2,1)S(1)}, u32[]{:S(2)}, u32[]{:S(2)}) %collective-permute-start.8) | collective-permute-done | bytes 497696 | tf_op jit(solution)/shard_map/ppermute | solution.py:35
  87.7 15.9 %collective-permute-done.9.refs_2_ = bf16[4,72,864]{2,1,0:T(8,128)(2,1)S(1)} collective-permute-done((bf16[4,72,864]{2,1,0:T(8,128)(2,1)S(1)}, bf16[4,72,864]{2,1,0:T(8,128)(2,1)S(1)}, u32[]{:S(2)}, u32[]{:S(2)}) %collective-permute-start.9) | collective-permute-done | bytes 497696 | tf_op jit(solution)/shard_map/ppermute | solution.py:35
  108.5 10.3 %shard_map.96 = (bf16[2,1840,128]{2,1,0:T(8,128)(2,1)}, bf16[2,1840,128]{2,1,0:T(8,128)(2,1)}, bf16[2,1728,128]{2,1,0:T(8,128)(2,1)S(1)}, bf16[2,1728,128]{2,1,0:T(8,128)(2,1)S(1)}) custom-call(s32[2]{0:T(128)S(1)} %pad_add_fusion.where, bf16[4,864,864]{2,1,0:T(8,128)(2,1)} %bitcast.177, bf16[4,72,864]{2,1,0:T(8,128)(2,1)S(1)} %get-tuple-element.111.refs_0_, ...), custom_call_target="tpu_custom_call" | custom-call | flops 3057647616 | bytes 10395648 | tf_op jit(solution)/shard_map/pallas_call | solution.py:328
  119.8 5.4 %collective-permute-done.24 = bf16[4,72,1280]{2,1,0:T(8,128)(2,1)S(1)} collective-permute-done((bf16[4,72,1280]{2,1,0:T(8,128)(2,1)S(1)}, bf16[4,72,1280]{2,1,0:T(8,128)(2,1)S(1)}, u32[]{:S(2)}, u32[]{:S(2)}) %collective-permute-start.24) | collective-permute-done | bytes 737312 | tf_op jit(solution)/shard_map/ppermute | solution.py:35
  125.2 14.2 %collective-permute-done.23 = bf16[4,72,1280]{2,1,0:T(8,128)(2,1)S(1)} collective-permute-done((bf16[4,72,1280]{2,1,0:T(8,128)(2,1)S(1)}, bf16[4,72,1280]{2,1,0:T(8,128)(2,1)S(1)}, u32[]{:S(2)}, u32[]{:S(2)}) %collective-permute-start.23) | collective-permute-done | bytes 737312 | tf_op jit(solution)/shard_map/ppermute | solution.py:35
  151.4 8.6 %shard_map.97 = (bf16[2,1728,128]{2,1,0:T(8,128)(2,1)S(1)}, bf16[2,1728,128]{2,1,0:T(8,128)(2,1)S(1)}, bf16[2,1728,128]{2,1,0:T(8,128)(2,1)}, bf16[2,1728,128]{2,1,0:T(8,128)(2,1)}) custom-call(s32[2]{0:T(128)S(1)} %pad_add_fusion.where, bf16[4,864,864]{2,1,0:T(8,128)(2,1)} %bitcast.178, bf16[4,72,864]{2,1,0:T(8,128)(2,1)S(1)} %copy-done.13, ...), custom_call_target="tpu_custom_call" | custom-call | flops 3057647616 | bytes 10395648 | tf_op jit(solution)/shard_map/pallas_call | solution.py:328
  160.1 4.3 collective-permute-done.16
  167.5 1.9 fusion.12
  173.0 8.8 %shard_map.99 = (bf16[2,1728,128]{2,1,0:T(8,128)(2,1)}, bf16[2,1728,128]{2,1,0:T(8,128)(2,1)S(1)}, bf16[2,1728,128]{2,1,0:T(8,128)(2,1)}, bf16[2,1728,128]{2,1,0:T(8,128)(2,1)}) custom-call(s32[2]{0:T(128)S(1)} %pad_add_fusion.where, bf16[4,864,864]{2,1,0:T(8,128)(2,1)} %bitcast.179, bf16[4,72,864]{2,1,0:T(8,128)(2,1)S(1)} %copy-done.13, ...), custom_call_target="tpu_custom_call" | custom-call | flops 3057647616 | bytes 10395648 | tf_op jit(solution)/shard_map/pallas_call | solution.py:328
  183.1 21.4 %shard_map.98 = (bf16[2,17,320,128]{3,2,1,0:T(8,128)(2,1)S(1)}, f32[16,8,256]{2,1,0:T(8,128)S(1)}) custom-call(s32[2]{0:T(128)S(1)} %pad_add_fusion.where, bf16[1,320,640]{2,1,0:T(8,128)(2,1)S(1)} %copy-done.42, bf16[1,320,640]{2,1,0:T(8,128)(2,1)} %collective-permute-done.4.refs_1_, bf16[1,320,640]{2,1,0:T(8,128)(2,1)} %collective-permute-done.5.refs_2_, ...), custom_call_target="tpu_custom_call" | custom-call | flops 3565158400 | bytes 10453000 | tf_op jit(solution)/shard_map/pallas_call | solution.py:67
  209.8 1.8 maximum_select_fusion
  215.0 14.5 %collective-permute-start.29 = (bf16[1840,128]{1,0:T(8,128)(2,1)}, bf16[1840,128]{1,0:T(8,128)(2,1)S(1)}, u32[]{:S(2)}, u32[]{:S(2)}) collective-permute-start(bf16[1840,128]{1,0:T(8,128)(2,1)} %pad_maximum_fusion.8), channel_id=1, source_target_pairs={{0,8},{2,10},{4,12},{6,14},{8,0},{10,2},{12,4},{14,6},{16,24},{18,... | collective-permute-start | bytes 1413128 | tf_op jit(solution)/shard_map/ppermute | solution.py:35
  238.8 8.6 %shard_map.100 = (bf16[2,1728,128]{2,1,0:T(8,128)(2,1)S(1)}, bf16[2,1728,128]{2,1,0:T(8,128)(2,1)S(1)}, bf16[2,1728,128]{2,1,0:T(8,128)(2,1)}, bf16[2,1728,128]{2,1,0:T(8,128)(2,1)}) custom-call(s32[2]{0:T(128)S(1)} %pad_add_fusion.where, bf16[4,864,864]{2,1,0:T(8,128)(2,1)} %bitcast.180, bf16[4,72,864]{2,1,0:T(8,128)(2,1)S(1)} %copy-done.13, ...), custom_call_target="tpu_custom_call" | custom-call | flops 3057647616 | bytes 10395648 | tf_op jit(solution)/shard_map/pallas_call | solution.py:328
  249.9 8.2 %collective-permute-done.29 = bf16[1840,128]{1,0:T(8,128)(2,1)S(1)} collective-permute-done((bf16[1840,128]{1,0:T(8,128)(2,1)}, bf16[1840,128]{1,0:T(8,128)(2,1)S(1)}, u32[]{:S(2)}, u32[]{:S(2)}) %collective-permute-start.29) | collective-permute-done | bytes 471072 | tf_op jit(solution)/shard_map/ppermute | solution.py:35
  260.7 1.8 collective-permute-start.32
  265.1 18.6 %collective-permute-done.33 = bf16[976,128]{1,0:T(8,128)(2,1)S(1)} collective-permute-done((bf16[976,128]{1,0:T(8,128)(2,1)S(1)}, bf16[976,128]{1,0:T(8,128)(2,1)S(1)}, u32[]{:S(2)}, u32[]{:S(2)}) %collective-permute-start.33) | collective-permute-done | bytes 249888 | tf_op jit(solution)/shard_map/ppermute | solution.py:35
  285.2 12.7 %collective-permute-done.32 = bf16[2,864,128]{2,1,0:T(8,128)(2,1)S(1)} collective-permute-done((bf16[2,864,128]{2,1,0:T(8,128)(2,1)S(1)}, bf16[2,864,128]{2,1,0:T(8,128)(2,1)S(1)}, u32[]{:S(2)}, u32[]{:S(2)}) %collective-permute-start.32) | collective-permute-done | bytes 442400 | tf_op jit(solution)/shard_map/ppermute | solution.py:35
  299.3 5.9 %collective-permute-done.37 = bf16[2,1728,128]{2,1,0:T(8,128)(2,1)} collective-permute-done((bf16[2,1728,128]{2,1,0:T(8,128)(2,1)S(1)}, bf16[2,1728,128]{2,1,0:T(8,128)(2,1)}, u32[]{:S(2)}, u32[]{:S(2)}) %collective-permute-start.37) | collective-permute-done | bytes 884768 | tf_op jit(solution)/shard_map/ppermute | solution.py:35
  306.6 2.9 collective-permute-start.39
  312.6 10.8 %collective-permute-done.38 = bf16[1,864,128]{2,1,0:T(8,128)(2,1)S(1)} collective-permute-done((bf16[1,864,128]{2,1,0:T(8,128)(2,1)S(1)}, bf16[1,864,128]{2,1,0:T(8,128)(2,1)S(1)}, u32[]{:S(2)}, u32[]{:S(2)}) %collective-permute-start.38) | collective-permute-done | bytes 221216 | tf_op jit(solution)/shard_map/ppermute | solution.py:35
  323.4 4.6 collective-permute-done.39
  328.7 3.3 collective-permute-done.40
  333.6 2.0 collective-permute-start.46
  335.9 2.9 collective-permute-start.47
  338.9 23.0 %collective-permute-done.43 = bf16[16,128]{1,0:T(8,128)(2,1)S(1)} collective-permute-done((bf16[16,128]{1,0:T(8,128)(2,1)S(1)}, bf16[16,128]{1,0:T(8,128)(2,1)S(1)}, u32[]{:S(2)}, u32[]{:S(2)}) %collective-permute-start.43) | collective-permute-done | bytes 4128 | tf_op jit(solution)/shard_map/ppermute | solution.py:35
  364.6 2.9 collective-permute-done.48.refs_1_.refs_3_
  372.5 13.1 %shard_map.101 = f32[4,2,128]{2,1,0:T(2,128)S(1)} custom-call(s32[2]{0:T(128)S(1)} %pad_add_fusion.where, bf16[4,864,128]{2,1,0:T(8,128)(2,1)S(1)} %bitcast.172, f32[864,1280]{1,0:T(8,128)} %copy-done, f32[864,128]{1,0:T(8,128)S(1)} %pad_convert_fusion.query_b, f32[16,8,256]{2,1,0:T(8,128)S(1)} %get-tuple-element.174.info, ...), custom_call_target="tpu_custom_call" | custom-call | flops 18119393280 | bytes 8093696 | tf_op jit(solution)/shard_map/pallas_call | solution.py:391
  385.7 5.0 %collective-permute-done.52 = bf16[1,864,128]{2,1,0:T(8,128)(2,1)S(1)} collective-permute-done((bf16[1,864,128]{2,1,0:T(8,128)(2,1)S(1)}, bf16[1,864,128]{2,1,0:T(8,128)(2,1)S(1)}, u32[]{:S(2)}, u32[]{:S(2)}) %collective-permute-start.52) | collective-permute-done | bytes 221216 | tf_op jit(solution)/shard_map/ppermute | solution.py:35
  391.2 3.5 collective-permute-start.55
  395.0 12.8 %shard_map.102 = f32[4,2,128]{2,1,0:T(2,128)S(1)} custom-call(s32[2]{0:T(128)S(1)} %pad_add_fusion.where, bf16[4,864,128]{2,1,0:T(8,128)(2,1)S(1)} %bitcast.174, f32[864,1280]{1,0:T(8,128)} %copy-done, f32[864,128]{1,0:T(8,128)S(1)} %pad_convert_fusion.query_b, f32[16,8,256]{2,1,0:T(8,128)S(1)} %get-tuple-element.174.info, ...), custom_call_target="tpu_custom_call" | custom-call | flops 18119393280 | bytes 8093696 | tf_op jit(solution)/shard_map/pallas_call | solution.py:391
  412.9 12.7 %shard_map.103 = f32[4,2,128]{2,1,0:T(2,128)S(1)} custom-call(s32[2]{0:T(128)S(1)} %pad_add_fusion.where, bf16[4,864,128]{2,1,0:T(8,128)(2,1)S(1)} %bitcast.175, f32[864,1280]{1,0:T(8,128)} %copy-done, f32[864,128]{1,0:T(8,128)S(1)} %pad_convert_fusion.query_b, f32[16,8,256]{2,1,0:T(8,128)S(1)} %get-tuple-element.174.info, ...), custom_call_target="tpu_custom_call" | custom-call | flops 18119393280 | bytes 8093696 | tf_op jit(solution)/shard_map/pallas_call | solution.py:391
  425.7 12.9 %shard_map.104 = f32[4,2,128]{2,1,0:T(2,128)S(1)} custom-call(s32[2]{0:T(128)S(1)} %pad_add_fusion.where, bf16[4,864,128]{2,1,0:T(8,128)(2,1)S(1)} %bitcast.173, f32[864,1280]{1,0:T(8,128)} %copy-done, f32[864,128]{1,0:T(8,128)S(1)} %pad_convert_fusion.query_b, f32[16,8,256]{2,1,0:T(8,128)S(1)} %get-tuple-element.174.info, ...), custom_call_target="tpu_custom_call" | custom-call | flops 18119393280 | bytes 8093696 | tf_op jit(solution)/shard_map/pallas_call | solution.py:391
  438.9 10.8 %all_to_all.5 = f32[16,2,16]{2,1,0:T(2,128)S(1)} all-to-all(f32[16,2,16]{2,1,0:T(2,128)S(1)} %multiply_reduce_fusion), channel_id=1, replica_groups=mesh['seq'=16,'eig'=2] {'seq'}, dimensions={0} | all-to-all | bytes 4096 | tf_op jit(solution)/shard_map/all_to_all | solution.py:619
  (326 shorter events, 92.2 us)
Async XLA Ops:
  6.5 298.7 %reduce-scatter.2.cloned.1.call-start = ((), (), s32[]{:S(2)}) async-start(), calls=%async_computation.2 | async-start | bytes 3481600 | tf_op jit(solution)/shard_map/reduce_scatter | solution.py:543
  19.6 29.6 %collective-permute-start.3 = (bf16[72,4736]{1,0:T(8,128)(2,1)S(1)}, bf16[72,4736]{1,0:T(8,128)(2,1)S(1)}, u32[]{:S(2)}, u32[]{:S(2)}) collective-permute-start(bf16[72,4736]{1,0:T(8,128)(2,1)S(1)} %get-tuple-element.104), channel_id=1, source_target_pairs={{0,8},{2,10},{4,12},{6,14},{8,0},{10,2},{12,4},{14,6},{16,24},{18,... | collective-permute-start | bytes 2045960 | tf_op jit(solution)/shard_map/ppermute | solution.py:35
  21.2 30.1 %collective-permute-start.1 = (bf16[1,320,864]{2,1,0:T(8,128)(2,1)S(1)}, bf16[1,320,864]{2,1,0:T(8,128)(2,1)S(1)}, u32[]{:S(2)}, u32[]{:S(2)}) collective-permute-start(bf16[1,320,864]{2,1,0:T(8,128)(2,1)S(1)} %get-tuple-element.99), channel_id=1, source_target_pairs={{0,4},{2,6},{4,0},{6,2},{8,12},{10,14},{12,8},{14,10},{16,20},{18,... | collective-permute-start | bytes 1658888 | tf_op jit(solution)/shard_map/ppermute | solution.py:35
  22.7 48.6 %collective-permute-start.6 = (bf16[72,4736]{1,0:T(8,128)(2,1)}, bf16[72,4736]{1,0:T(8,128)(2,1)S(1)}, u32[]{:S(2)}, u32[]{:S(2)}) collective-permute-start(bf16[72,4736]{1,0:T(8,128)(2,1)} %get-tuple-element.109), channel_id=1, source_target_pairs={{0,16},{2,18},{4,20},{6,22},{8,24},{10,26},{12,28},{14,30},{16,0},... | collective-permute-start | bytes 2045960 | tf_op jit(solution)/shard_map/ppermute | solution.py:35
  25.3 46.0 %collective-permute-start.7 = (bf16[72,4736]{1,0:T(8,128)(2,1)}, bf16[72,4736]{1,0:T(8,128)(2,1)S(1)}, u32[]{:S(2)}, u32[]{:S(2)}) collective-permute-start(bf16[72,4736]{1,0:T(8,128)(2,1)} %get-tuple-element.110), channel_id=1, source_target_pairs={{0,24},{2,26},{4,28},{6,30},{8,16},{10,18},{12,20},{14,22},{16,8},... | collective-permute-start | bytes 2045960 | tf_op jit(solution)/shard_map/ppermute | solution.py:35
  33.4 28.3 %collective-permute-start.2 = (bf16[1,320,864]{2,1,0:T(8,128)(2,1)}, bf16[1,320,864]{2,1,0:T(8,128)(2,1)}, u32[]{:S(2)}, u32[]{:S(2)}) collective-permute-start(bf16[1,320,864]{2,1,0:T(8,128)(2,1)} %get-tuple-element.101), channel_id=1, source_target_pairs={{0,6},{2,4},{4,2},{6,0},{8,14},{10,12},{12,10},{14,8},{16,22},{18,... | collective-permute-start | bytes 1658888 | tf_op jit(solution)/shard_map/ppermute | solution.py:35
  49.2 20.2 %collective-permute-start.5 = (bf16[1,320,640]{2,1,0:T(8,128)(2,1)}, bf16[1,320,640]{2,1,0:T(8,128)(2,1)}, u32[]{:S(2)}, u32[]{:S(2)}) collective-permute-start(bf16[1,320,640]{2,1,0:T(8,128)(2,1)} %get-tuple-element.107), channel_id=1, source_target_pairs={{0,4},{2,6},{4,0},{6,2},{8,12},{10,14},{12,8},{14,10},{16,20},{18,... | collective-permute-start | bytes 1228808 | tf_op jit(solution)/shard_map/ppermute | solution.py:35
  52.1 17.4 %collective-permute-start.4 = (bf16[1,320,640]{2,1,0:T(8,128)(2,1)}, bf16[1,320,640]{2,1,0:T(8,128)(2,1)}, u32[]{:S(2)}, u32[]{:S(2)}) collective-permute-start(bf16[1,320,640]{2,1,0:T(8,128)(2,1)} %get-tuple-element.105), channel_id=1, source_target_pairs={{0,2},{2,0},{4,6},{6,4},{8,10},{10,8},{12,14},{14,12},{16,18},{18,... | collective-permute-start | bytes 1228808 | tf_op jit(solution)/shard_map/ppermute | solution.py:35
  73.0 30.6 %collective-permute-start.9 = (bf16[4,72,864]{2,1,0:T(8,128)(2,1)S(1)}, bf16[4,72,864]{2,1,0:T(8,128)(2,1)S(1)}, u32[]{:S(2)}, u32[]{:S(2)}) collective-permute-start(bf16[4,72,864]{2,1,0:T(8,128)(2,1)S(1)} %get-tuple-element.113), channel_id=1, source_target_pairs={{0,4},{2,6},{4,0},{6,2},{8,12},{10,14},{12,8},{14,10},{16,20},{18,... | collective-permute-start | bytes 1493000 | tf_op jit(solution)/shard_map/ppermute | solution.py:35
  73.5 30.1 %collective-permute-start.10 = (bf16[4,72,864]{2,1,0:T(8,128)(2,1)S(1)}, bf16[4,72,864]{2,1,0:T(8,128)(2,1)S(1)}, u32[]{:S(2)}, u32[]{:S(2)}) collective-permute-start(bf16[4,72,864]{2,1,0:T(8,128)(2,1)S(1)} %get-tuple-element.114), channel_id=1, source_target_pairs={{0,6},{2,4},{4,2},{6,0},{8,14},{10,12},{12,10},{14,8},{16,22},{18,... | collective-permute-start | bytes 1493000 | tf_op jit(solution)/shard_map/ppermute | solution.py:35
  76.0 29.6 %collective-permute-start.11 = (bf16[4,72,864]{2,1,0:T(8,128)(2,1)S(1)}, bf16[4,72,864]{2,1,0:T(8,128)(2,1)S(1)}, u32[]{:S(2)}, u32[]{:S(2)}) collective-permute-start(bf16[4,72,864]{2,1,0:T(8,128)(2,1)S(1)} %get-tuple-element.111.refs_0_), channel_id=1, source_target_pairs={{0,1},{1,0},{2,3},{3,2},{4,5},{5,4},{6,7},{7,6},{8,9},{9,8},{10,11... | collective-permute-start | bytes 1493000 | tf_op jit(solution)/shard_map/ppermute | solution.py:35
  87.2 19.7 %collective-permute-start.12 = (bf16[4,72,864]{2,1,0:T(8,128)(2,1)S(1)}, bf16[4,72,864]{2,1,0:T(8,128)(2,1)S(1)}, u32[]{:S(2)}, u32[]{:S(2)}) collective-permute-start(bf16[4,72,864]{2,1,0:T(8,128)(2,1)S(1)} %collective-permute-done.8.refs_1_), channel_id=1, source_target_pairs={{0,1},{1,0},{2,3},{3,2},{4,5},{5,4},{6,7},{7,6},{8,9},{9,8},{10,11... | collective-permute-start | bytes 1493000 | tf_op jit(solution)/shard_map/ppermute | solution.py:35
  87.2 16.9 %collective-permute-start.21 = (bf16[1,320,640]{2,1,0:T(8,128)(2,1)S(1)}, bf16[1,320,640]{2,1,0:T(8,128)(2,1)S(1)}, u32[]{:S(2)}, u32[]{:S(2)}) collective-permute-start(bf16[1,320,640]{2,1,0:T(8,128)(2,1)S(1)} %copy-done.46), channel_id=1, source_target_pairs={{0,6},{2,4},{4,2},{6,0},{8,14},{10,12},{12,10},{14,8},{16,22},{18,... | collective-permute-start | bytes 1228808 | tf_op jit(solution)/shard_map/ppermute | solution.py:35
  104.9 20.3 %collective-permute-start.24 = (bf16[4,72,1280]{2,1,0:T(8,128)(2,1)S(1)}, bf16[4,72,1280]{2,1,0:T(8,128)(2,1)S(1)}, u32[]{:S(2)}, u32[]{:S(2)}) collective-permute-start(bf16[4,72,1280]{2,1,0:T(8,128)(2,1)S(1)} %get-tuple-element.133), channel_id=1, source_target_pairs={{0,6},{2,4},{4,2},{6,0},{8,14},{10,12},{12,10},{14,8},{16,22},{18,... | collective-permute-start | bytes 2211848 | tf_op jit(solution)/shard_map/ppermute | solution.py:35
  105.6 33.8 %collective-permute-start.23 = (bf16[4,72,1280]{2,1,0:T(8,128)(2,1)S(1)}, bf16[4,72,1280]{2,1,0:T(8,128)(2,1)S(1)}, u32[]{:S(2)}, u32[]{:S(2)}) collective-permute-start(bf16[4,72,1280]{2,1,0:T(8,128)(2,1)S(1)} %get-tuple-element.133), channel_id=1, source_target_pairs={{0,4},{2,6},{4,0},{6,2},{8,12},{10,14},{12,8},{14,10},{16,20},{18,... | collective-permute-start | bytes 2211848 | tf_op jit(solution)/shard_map/ppermute | solution.py:35
  106.9 32.5 %collective-permute-start.22 = (bf16[4,72,1280]{2,1,0:T(8,128)(2,1)S(1)}, bf16[4,72,1280]{2,1,0:T(8,128)(2,1)S(1)}, u32[]{:S(2)}, u32[]{:S(2)}) collective-permute-start(bf16[4,72,1280]{2,1,0:T(8,128)(2,1)S(1)} %get-tuple-element.133), channel_id=1, source_target_pairs={{0,2},{2,0},{4,6},{6,4},{8,10},{10,8},{12,14},{14,12},{16,18},{18,... | collective-permute-start | bytes 2211848 | tf_op jit(solution)/shard_map/ppermute | solution.py:35
  142.2 40.9 %collective-permute-start.25 = (bf16[16,72,1280]{2,1,0:T(8,128)(2,1)}, bf16[16,72,1280]{2,1,0:T(8,128)(2,1)}, u32[]{:S(2)}, u32[]{:S(2)}) collective-permute-start(bf16[16,72,1280]{2,1,0:T(8,128)(2,1)} %constant_dynamic-update-slice_fusion.refs_4_), channel_id=1, source_target_pairs={{0,1},{1,0},{2,3},{3,2},{4,5},{5,4},{6,7},{7,6},{8,9},{9,8},{10,11... | collective-permute-start | bytes 8847368 | tf_op jit(solution)/shard_map/ppermute | solution.py:35
  142.2 22.2 %collective-permute-start.16 = (bf16[2,1728,128]{2,1,0:T(8,128)(2,1)S(1)}, bf16[2,1728,128]{2,1,0:T(8,128)(2,1)}, u32[]{:S(2)}, u32[]{:S(2)}) collective-permute-start(bf16[2,1728,128]{2,1,0:T(8,128)(2,1)S(1)} %get-tuple-element.115), channel_id=1, source_target_pairs={{0,4},{2,6},{4,0},{6,2},{8,12},{10,14},{12,8},{14,10},{16,20},{18,... | collective-permute-start | bytes 2654216 | tf_op jit(solution)/shard_map/ppermute | solution.py:35
  143.6 23.3 %collective-permute-start.15 = (bf16[2,1840,128]{2,1,0:T(8,128)(2,1)}, bf16[2,1840,128]{2,1,0:T(8,128)(2,1)}, u32[]{:S(2)}, u32[]{:S(2)}) collective-permute-start(bf16[2,1840,128]{2,1,0:T(8,128)(2,1)} %get-tuple-element.119), channel_id=1, source_target_pairs={{0,2},{2,0},{4,6},{6,4},{8,10},{10,8},{12,14},{14,12},{16,18},{18,... | collective-permute-start | bytes 2826248 | tf_op jit(solution)/shard_map/ppermute | solution.py:35
  169.4 35.7 %collective-permute-start.18 = (bf16[1840,128]{1,0:T(8,128)(2,1)}, bf16[1840,128]{1,0:T(8,128)(2,1)S(1)}, u32[]{:S(2)}, u32[]{:S(2)}) collective-permute-start(bf16[1840,128]{1,0:T(8,128)(2,1)} %fusion.12), channel_id=1, source_target_pairs={{0,4},{2,6},{4,0},{6,2},{8,12},{10,14},{12,8},{14,10},{16,20},{18,... | collective-permute-start | bytes 1413128 | tf_op jit(solution)/shard_map/ppermute | solution.py:35
  170.9 40.9 %collective-permute-start.20 = (bf16[2,1728,128]{2,1,0:T(8,128)(2,1)}, bf16[2,1728,128]{2,1,0:T(8,128)(2,1)}, u32[]{:S(2)}, u32[]{:S(2)}) collective-permute-start(bf16[2,1728,128]{2,1,0:T(8,128)(2,1)} %get-tuple-element.126), channel_id=1, source_target_pairs={{0,4},{2,6},{4,0},{6,2},{8,12},{10,14},{12,8},{14,10},{16,20},{18,... | collective-permute-start | bytes 2654216 | tf_op jit(solution)/shard_map/ppermute | solution.py:35
  171.5 36.9 %collective-permute-start.17 = (bf16[2,1728,128]{2,1,0:T(8,128)(2,1)S(1)}, bf16[2,1728,128]{2,1,0:T(8,128)(2,1)S(1)}, u32[]{:S(2)}, u32[]{:S(2)}) collective-permute-start(bf16[2,1728,128]{2,1,0:T(8,128)(2,1)S(1)} %get-tuple-element.121), channel_id=1, source_target_pairs={{0,2},{2,0},{4,6},{6,4},{8,10},{10,8},{12,14},{14,12},{16,18},{18,... | collective-permute-start | bytes 2654216 | tf_op jit(solution)/shard_map/ppermute | solution.py:35
  211.7 150.3 %all-gather.2.cloned.1.call-start = ((), (), s32[]{:S(2)}) async-start(), calls=%async_computation.3 | async-start | bytes 3481600 | tf_op jit(solution)/shard_map/all_gather | solution.py:586
  211.7 35.6 %collective-permute-start.27 = (bf16[1728,128]{1,0:T(8,128)(2,1)}, bf16[1728,128]{1,0:T(8,128)(2,1)S(1)}, u32[]{:S(2)}, u32[]{:S(2)}) collective-permute-start(bf16[1728,128]{1,0:T(8,128)(2,1)} %fusion.13), channel_id=1, source_target_pairs={{0,4},{2,6},{4,0},{6,2},{8,12},{10,14},{12,8},{14,10},{16,20},{18,... | collective-permute-start | bytes 1327112 | tf_op jit(solution)/shard_map/ppermute | solution.py:35
  214.0 33.5 %collective-permute-start.28 = (bf16[1728,128]{1,0:T(8,128)(2,1)S(1)}, bf16[1728,128]{1,0:T(8,128)(2,1)S(1)}, u32[]{:S(2)}, u32[]{:S(2)}) collective-permute-start(bf16[1728,128]{1,0:T(8,128)(2,1)S(1)} %fusion.15), channel_id=1, source_target_pairs={{0,2},{2,0},{4,6},{6,4},{8,10},{10,8},{12,14},{14,12},{16,18},{18,... | collective-permute-start | bytes 1327112 | tf_op jit(solution)/shard_map/ppermute | solution.py:35
  215.0 43.1 %collective-permute-start.29 = (bf16[1840,128]{1,0:T(8,128)(2,1)}, bf16[1840,128]{1,0:T(8,128)(2,1)S(1)}, u32[]{:S(2)}, u32[]{:S(2)}) collective-permute-start(bf16[1840,128]{1,0:T(8,128)(2,1)} %pad_maximum_fusion.8), channel_id=1, source_target_pairs={{0,8},{2,10},{4,12},{6,14},{8,0},{10,2},{12,4},{14,6},{16,24},{18,... | collective-permute-start | bytes 1413128 | tf_op jit(solution)/shard_map/ppermute | solution.py:35
  229.5 29.6 %collective-permute-start.31 = (bf16[2,1728,128]{2,1,0:T(8,128)(2,1)}, bf16[2,1728,128]{2,1,0:T(8,128)(2,1)S(1)}, u32[]{:S(2)}, u32[]{:S(2)}) collective-permute-start(bf16[2,1728,128]{2,1,0:T(8,128)(2,1)} %get-tuple-element.146), channel_id=1, source_target_pairs={{0,4},{2,6},{4,0},{6,2},{8,12},{10,14},{12,8},{14,10},{16,20},{18,... | collective-permute-start | bytes 2654216 | tf_op jit(solution)/shard_map/ppermute | solution.py:35
  230.6 28.6 %collective-permute-start.30 = (bf16[2,1728,128]{2,1,0:T(8,128)(2,1)}, bf16[2,1728,128]{2,1,0:T(8,128)(2,1)S(1)}, u32[]{:S(2)}, u32[]{:S(2)}) collective-permute-start(bf16[2,1728,128]{2,1,0:T(8,128)(2,1)} %get-tuple-element.145), channel_id=1, source_target_pairs={{0,2},{2,0},{4,6},{6,4},{8,10},{10,8},{12,14},{14,12},{16,18},{18,... | collective-permute-start | bytes 2654216 | tf_op jit(solution)/shard_map/ppermute | solution.py:35
  259.2 24.5 %collective-permute-start.33 = (bf16[976,128]{1,0:T(8,128)(2,1)S(1)}, bf16[976,128]{1,0:T(8,128)(2,1)S(1)}, u32[]{:S(2)}, u32[]{:S(2)}) collective-permute-start(bf16[976,128]{1,0:T(8,128)(2,1)S(1)} %pad_maximum_fusion.13), channel_id=1, source_target_pairs={{0,16},{2,18},{4,20},{6,22},{8,24},{10,26},{12,28},{14,30},{16,0},... | collective-permute-start | bytes 749576 | tf_op jit(solution)/shard_map/ppermute | solution.py:35
  260.7 37.2 %collective-permute-start.32 = (bf16[2,864,128]{2,1,0:T(8,128)(2,1)S(1)}, bf16[2,864,128]{2,1,0:T(8,128)(2,1)S(1)}, u32[]{:S(2)}, u32[]{:S(2)}) collective-permute-start(bf16[2,864,128]{2,1,0:T(8,128)(2,1)S(1)} %dynamic-slice_bitcast_fusion.5), channel_id=1, source_target_pairs={{0,8},{2,10},{4,12},{6,14},{8,0},{10,2},{12,4},{14,6},{16,24},{18,... | collective-permute-start | bytes 1327112 | tf_op jit(solution)/shard_map/ppermute | solution.py:35
  262.8 35.3 %collective-permute-start.34 = (bf16[1728,128]{1,0:T(8,128)(2,1)S(1)}, bf16[1728,128]{1,0:T(8,128)(2,1)S(1)}, u32[]{:S(2)}, u32[]{:S(2)}) collective-permute-start(bf16[1728,128]{1,0:T(8,128)(2,1)S(1)} %fusion.16), channel_id=1, source_target_pairs={{0,4},{2,6},{4,0},{6,2},{8,12},{10,14},{12,8},{14,10},{16,20},{18,... | collective-permute-start | bytes 1327112 | tf_op jit(solution)/shard_map/ppermute | solution.py:35
  263.1 35.1 %collective-permute-start.35 = (bf16[1728,128]{1,0:T(8,128)(2,1)S(1)}, bf16[1728,128]{1,0:T(8,128)(2,1)S(1)}, u32[]{:S(2)}, u32[]{:S(2)}) collective-permute-start(bf16[1728,128]{1,0:T(8,128)(2,1)S(1)} %fusion.17), channel_id=1, source_target_pairs={{0,2},{2,0},{4,6},{6,4},{8,10},{10,8},{12,14},{14,12},{16,18},{18,... | collective-permute-start | bytes 1327112 | tf_op jit(solution)/shard_map/ppermute | solution.py:35
  263.5 34.9 %collective-permute-start.36 = (bf16[2,1728,128]{2,1,0:T(8,128)(2,1)S(1)}, bf16[2,1728,128]{2,1,0:T(8,128)(2,1)S(1)}, u32[]{:S(2)}, u32[]{:S(2)}) collective-permute-start(bf16[2,1728,128]{2,1,0:T(8,128)(2,1)S(1)} %get-tuple-element.156), channel_id=1, source_target_pairs={{0,2},{2,0},{4,6},{6,4},{8,10},{10,8},{12,14},{14,12},{16,18},{18,... | collective-permute-start | bytes 2654216 | tf_op jit(solution)/shard_map/ppermute | solution.py:35
  283.7 21.5 %collective-permute-start.37 = (bf16[2,1728,128]{2,1,0:T(8,128)(2,1)S(1)}, bf16[2,1728,128]{2,1,0:T(8,128)(2,1)}, u32[]{:S(2)}, u32[]{:S(2)}) collective-permute-start(bf16[2,1728,128]{2,1,0:T(8,128)(2,1)S(1)} %copy-done.61), channel_id=1, source_target_pairs={{0,4},{2,6},{4,0},{6,2},{8,12},{10,14},{12,8},{14,10},{16,20},{18,... | collective-permute-start | bytes 2654216 | tf_op jit(solution)/shard_map/ppermute | solution.py:35
  306.5 16.9 %collective-permute-start.38 = (bf16[1,864,128]{2,1,0:T(8,128)(2,1)S(1)}, bf16[1,864,128]{2,1,0:T(8,128)(2,1)S(1)}, u32[]{:S(2)}, u32[]{:S(2)}) collective-permute-start(bf16[1,864,128]{2,1,0:T(8,128)(2,1)S(1)} %constant_dynamic-slice_fusion.2), channel_id=1, source_target_pairs={{0,16},{2,18},{4,20},{6,22},{8,24},{10,26},{12,28},{14,30},{16,0},... | collective-permute-start | bytes 663560 | tf_op jit(solution)/shard_map/ppermute | solution.py:35
  306.6 21.4 %collective-permute-start.39 = (bf16[864,128]{1,0:T(8,128)(2,1)S(1)}, bf16[864,128]{1,0:T(8,128)(2,1)S(1)}, u32[]{:S(2)}, u32[]{:S(2)}) collective-permute-start(bf16[864,128]{1,0:T(8,128)(2,1)S(1)} %fusion.20), channel_id=1, source_target_pairs={{0,16},{2,18},{4,20},{6,22},{8,24},{10,26},{12,28},{14,30},{16,0},... | collective-permute-start | bytes 663560 | tf_op jit(solution)/shard_map/ppermute | solution.py:35
  310.7 18.0 %collective-permute-start.42 = (bf16[1728,128]{1,0:T(8,128)(2,1)S(1)}, bf16[1728,128]{1,0:T(8,128)(2,1)S(1)}, u32[]{:S(2)}, u32[]{:S(2)}) collective-permute-start(bf16[1728,128]{1,0:T(8,128)(2,1)S(1)} %fusion.19), channel_id=1, source_target_pairs={{0,2},{2,0},{4,6},{6,4},{8,10},{10,8},{12,14},{14,12},{16,18},{18,... | collective-permute-start | bytes 1327112 | tf_op jit(solution)/shard_map/ppermute | solution.py:35
  312.4 19.6 %collective-permute-start.40 = (bf16[2,864,128]{2,1,0:T(8,128)(2,1)S(1)}, bf16[2,864,128]{2,1,0:T(8,128)(2,1)S(1)}, u32[]{:S(2)}, u32[]{:S(2)}) collective-permute-start(bf16[2,864,128]{2,1,0:T(8,128)(2,1)S(1)} %dynamic-slice_bitcast_fusion.4), channel_id=1, source_target_pairs={{0,8},{2,10},{4,12},{6,14},{8,0},{10,2},{12,4},{14,6},{16,24},{18,... | collective-permute-start | bytes 1327112 | tf_op jit(solution)/shard_map/ppermute | solution.py:35
  312.4 19.6 %collective-permute-start.41 = (bf16[1728,128]{1,0:T(8,128)(2,1)S(1)}, bf16[1728,128]{1,0:T(8,128)(2,1)S(1)}, u32[]{:S(2)}, u32[]{:S(2)}) collective-permute-start(bf16[1728,128]{1,0:T(8,128)(2,1)S(1)} %fusion.18), channel_id=1, source_target_pairs={{0,4},{2,6},{4,0},{6,2},{8,12},{10,14},{12,8},{14,10},{16,20},{18,... | collective-permute-start | bytes 1327112 | tf_op jit(solution)/shard_map/ppermute | solution.py:35
  333.5 28.4 %collective-permute-start.44 = (bf16[1712,128]{1,0:T(8,128)(2,1)S(1)}, bf16[1712,128]{1,0:T(8,128)(2,1)S(1)}, u32[]{:S(2)}, u32[]{:S(2)}) collective-permute-start(bf16[1712,128]{1,0:T(8,128)(2,1)S(1)} %pad_maximum_fusion.12), channel_id=1, source_target_pairs={{0,8},{2,10},{4,12},{6,14},{8,0},{10,2},{12,4},{14,6},{16,24},{18,... | collective-permute-start | bytes 1314824 | tf_op jit(solution)/shard_map/ppermute | solution.py:35
  333.6 28.3 %collective-permute-start.46 = (bf16[2,864,128]{2,1,0:T(8,128)(2,1)S(1)}, bf16[2,864,128]{2,1,0:T(8,128)(2,1)S(1)}, u32[]{:S(2)}, u32[]{:S(2)}) collective-permute-start(bf16[2,864,128]{2,1,0:T(8,128)(2,1)S(1)} %dynamic-slice_bitcast_fusion.3), channel_id=1, source_target_pairs={{0,8},{2,10},{4,12},{6,14},{8,0},{10,2},{12,4},{14,6},{16,24},{18,... | collective-permute-start | bytes 1327112 | tf_op jit(solution)/shard_map/ppermute | solution.py:35
  335.8 26.1 %collective-permute-start.45 = (bf16[864,128]{1,0:T(8,128)(2,1)S(1)}, bf16[864,128]{1,0:T(8,128)(2,1)S(1)}, u32[]{:S(2)}, u32[]{:S(2)}) collective-permute-start(bf16[864,128]{1,0:T(8,128)(2,1)S(1)} %bitcast.191), channel_id=1, source_target_pairs={{0,16},{2,18},{4,20},{6,22},{8,24},{10,26},{12,28},{14,30},{16,0},... | collective-permute-start | bytes 663560 | tf_op jit(solution)/shard_map/ppermute | solution.py:35
  335.9 26.0 %collective-permute-start.47 = (bf16[1,864,128]{2,1,0:T(8,128)(2,1)S(1)}, bf16[1,864,128]{2,1,0:T(8,128)(2,1)S(1)}, u32[]{:S(2)}, u32[]{:S(2)}) collective-permute-start(bf16[1,864,128]{2,1,0:T(8,128)(2,1)S(1)} %constant_dynamic-slice_fusion.1), channel_id=1, source_target_pairs={{0,16},{2,18},{4,20},{6,22},{8,24},{10,26},{12,28},{14,30},{16,0},... | collective-permute-start | bytes 663560 | tf_op jit(solution)/shard_map/ppermute | solution.py:35
  338.8 23.1 %collective-permute-start.43 = (bf16[16,128]{1,0:T(8,128)(2,1)S(1)}, bf16[16,128]{1,0:T(8,128)(2,1)S(1)}, u32[]{:S(2)}, u32[]{:S(2)}) collective-permute-start(bf16[16,128]{1,0:T(8,128)(2,1)S(1)} %slice_bitcast_fusion.2), channel_id=1, source_target_pairs={{0,8},{2,10},{4,12},{6,14},{8,0},{10,2},{12,4},{14,6},{16,24},{18,... | collective-permute-start | bytes 12296 | tf_op jit(solution)/shard_map/ppermute | solution.py:35
  368.3 22.6 %collective-permute-start.51 = (bf16[864,128]{1,0:T(8,128)(2,1)S(1)}, bf16[864,128]{1,0:T(8,128)(2,1)S(1)}, u32[]{:S(2)}, u32[]{:S(2)}) collective-permute-start(bf16[864,128]{1,0:T(8,128)(2,1)S(1)} %bitcast.195), channel_id=1, source_target_pairs={{0,16},{2,18},{4,20},{6,22},{8,24},{10,26},{12,28},{14,30},{16,0},... | collective-permute-start | bytes 663560 | tf_op jit(solution)/shard_map/ppermute | solution.py:35
  369.8 20.9 %collective-permute-start.52 = (bf16[1,864,128]{2,1,0:T(8,128)(2,1)S(1)}, bf16[1,864,128]{2,1,0:T(8,128)(2,1)S(1)}, u32[]{:S(2)}, u32[]{:S(2)}) collective-permute-start(bf16[1,864,128]{2,1,0:T(8,128)(2,1)S(1)} %constant_dynamic-slice_fusion), channel_id=1, source_target_pairs={{0,16},{2,18},{4,20},{6,22},{8,24},{10,26},{12,28},{14,30},{16,0},... | collective-permute-start | bytes 663560 | tf_op jit(solution)/shard_map/ppermute | solution.py:35
  371.3 20.0 %collective-permute-start.50 = (bf16[1712,128]{1,0:T(8,128)(2,1)S(1)}, bf16[1712,128]{1,0:T(8,128)(2,1)S(1)}, u32[]{:S(2)}, u32[]{:S(2)}) collective-permute-start(bf16[1712,128]{1,0:T(8,128)(2,1)S(1)} %pad_maximum_fusion.11), channel_id=1, source_target_pairs={{0,8},{2,10},{4,12},{6,14},{8,0},{10,2},{12,4},{14,6},{16,24},{18,... | collective-permute-start | bytes 1314824 | tf_op jit(solution)/shard_map/ppermute | solution.py:35
  391.2 16.7 %collective-permute-start.55 = (bf16[864,128]{1,0:T(8,128)(2,1)S(1)}, bf16[864,128]{1,0:T(8,128)(2,1)S(1)}, u32[]{:S(2)}, u32[]{:S(2)}) collective-permute-start(bf16[864,128]{1,0:T(8,128)(2,1)S(1)} %bitcast.198), channel_id=1, source_target_pairs={{0,16},{2,18},{4,20},{6,22},{8,24},{10,26},{12,28},{14,30},{16,0},... | collective-permute-start | bytes 663560 | tf_op jit(solution)/shard_map/ppermute | solution.py:35
  (75 other events, 544.5 us)
Sparse Core Ops, SparseCore 0:
  211.8 90.2 reduce-scatter.1
  305.3 44.8 all-gather.1
where the time goes:
time: 463 us; the launch traced here: 459 us
  waiting for transfers between devices  171 us (37%)
  Pallas kernels  120 us (26%)
  starting transfers between devices  74.2 us (16%)
  local copies, waits for them, and re-layouts  46.3 us (10%)
  other arithmetic  21.1 us (5%)
  between operations  15.5 us (3%)
  blocking collectives  10.8 us (2%)
    ppermute x59, waiting for transfers between devices, swap(): return lax.ppermute(x, axis, [(i, i ^ mask) for i in range(size)])  171 us
    ppermute x59, starting transfers between devices, swap(): return lax.ppermute(x, axis, [(i, i ^ mask) for i in range(size)])  74.2 us
    pallas_call x4, Pallas kernels, score(): pl.pallas_call(functools.partial(score_kernel, chunk, outer, masks, len(a...  51.4 us
    unnamed x128, local copies, waits for them, and re-layouts  43.7 us
    pallas_call x4, Pallas kernels, rotate_out(): pl.pallas_call(functools.partial(rotate_out_kernel, chunk, outer, query_r...  36.4 us
    pallas_call x6, Pallas kernels, call(): pl.pallas_call(kernel, out_shape=list(outs), in_specs=[SMEM] + [VMEM] * (...  31.7 us
    convert_element_type x26, other arithmetic, add(): return total.astype(BF16)  15.8 us
    all_to_all x1, blocking collectives, body(): lax.all_to_all(scores, 'seq', split_axis=0, concat_axis=0, tiled=True)  10.8 us
  transfers between devices with their start and end apart: 61, of which 25 were waited for; matrix products, arithmetic and copies ran while one was open for 7% of the time, Pallas kernels for 22%

commit v1 on v0

--- a/solution.py
+++ b/solution.py
@@ -339,7 +339,7 @@
                 pltpu.VMEM((total, depth), F32),
             ],
         ),
-        compiler_params=pltpu.CompilerParams(vmem_limit_bytes=48 << 20),
+        compiler_params=pltpu.CompilerParams(vmem_limit_bytes=32 << 20),
         cost_estimate=pl.CostEstimate(
             flops=2 * outer * TOK_DEV * basis.size,
             bytes_accessed=2 * (basis.size + outer * TOK_DEV * (INNER * cols + depth)),
@@ -400,7 +400,7 @@
         * len(a_parts),
         out_specs=VMEM,
         scratch_shapes=[pltpu.VMEM((count + 1, rows, TOK_DEV), BF16)],
-        compiler_params=pltpu.CompilerParams(vmem_limit_bytes=48 << 20),
+        compiler_params=pltpu.CompilerParams(vmem_limit_bytes=28 << 20),
         cost_estimate=pl.CostEstimate(
             flops=16 * count * SEQ_DEV * TOK_DEV * cols * rows,
             bytes_accessed=2 * (b.size + a_parts[0].size + 2 * inverse.size),

time: 463 us -> 457 us (0.987)
  Pallas kernels: 120 us -> 106 us
  local copies, waits for them, and re-layouts: 46.3 us -> 55.1 us
    pallas_call x4, Pallas kernels: 36.4 us -> 27.2 us  [rotate_out(): pl.pallas_call(functools.partial(rotate_out_kernel, chunk, outer, query_r...]
    unnamed x128 -> x146, local copies, waits for them, and re-layouts: 43.7 us -> 52.7 us
  transfers between devices with their start and end apart: 61 -> 61, of which waited for: 25 -> 26; matrix products, arithmetic and copies ran while one was open for 7% -> 7% of each run, Pallas kernels for 22% -> 20%
where the time goes in v1:
time: 457 us; the launch traced here: 452 us
  waiting for transfers between devices  170 us (37%)
  Pallas kernels  106 us (23%)
  starting transfers between devices  74.2 us (16%)
  local copies, waits for them, and re-layouts  55.1 us (12%)
  other arithmetic  20.2 us (4%)
  between operations  15.6 us (3%)
  blocking collectives  10.7 us (2%)
    ppermute x59, waiting for transfers between devices, swap(): return lax.ppermute(x, axis, [(i, i ^ mask) for i in range(size)])  170 us
    ppermute x59, starting transfers between devices, swap(): return lax.ppermute(x, axis, [(i, i ^ mask) for i in range(size)])  74.1 us
    unnamed x146, local copies, waits for them, and re-layouts  52.7 us
    pallas_call x4, Pallas kernels, score(): pl.pallas_call(functools.partial(score_kernel, chunk, outer, masks, len(a...  47.2 us
    pallas_call x6, Pallas kernels, call(): pl.pallas_call(kernel, out_shape=list(outs), in_specs=[SMEM] + [VMEM] * (...  31.9 us
    pallas_call x4, Pallas kernels, rotate_out(): pl.pallas_call(functools.partial(rotate_out_kernel, chunk, outer, query_r...  27.2 us
    convert_element_type x26, other arithmetic, add(): return total.astype(BF16)  13.7 us
    all_to_all x1, blocking collectives, body(): lax.all_to_all(scores, 'seq', split_axis=0, concat_axis=0, tiled=True)  10.7 us
  transfers between devices with their start and end apart: 61, of which 26 were waited for; matrix products, arithmetic and copies ran while one was open for 7% of the time, Pallas kernels for 20%

profile of v1, /device:TPU:0, one launch (start us, length us, event | category | flops | bytes accessed | tf_op | source)
XLA Modules:
  0.0 452.4 jit_solution(987773169068701084)
XLA Ops:
  8.0 2.0 copy-done.5
  12.8 1.9 shard_map.91
  14.7 1.9 shard_map.92
  16.7 2.9 collective-permute-start
  22.7 2.6 collective-permute-start.6
  25.5 7.1 %collective-permute-done.refs_1_ = bf16[1,320,864]{2,1,0:T(8,128)(2,1)S(1)} collective-permute-done((bf16[1,320,864]{2,1,0:T(8,128)(2,1)S(1)}, bf16[1,320,864]{2,1,0:T(8,128)(2,1)S(1)}, u32[]{:S(2)}, u32[]{:S(2)}) %collective-permute-start) | collective-permute-done | bytes 552992 | tf_op jit(solution)/shard_map/ppermute | solution.py:35
  33.4 2.7 collective-permute-start.2
  39.5 9.7 %collective-permute-done.3.refs_1_ = bf16[72,4736]{1,0:T(8,128)(2,1)S(1)} collective-permute-done((bf16[72,4736]{1,0:T(8,128)(2,1)S(1)}, bf16[72,4736]{1,0:T(8,128)(2,1)S(1)}, u32[]{:S(2)}, u32[]{:S(2)}) %collective-permute-start.3) | collective-permute-done | bytes 682016 | tf_op jit(solution)/shard_map/ppermute | solution.py:35
  49.2 2.0 collective-permute-start.5
  52.6 9.2 %copy.64 = bf16[864,3456]{0,1:T(8,128)(2,1)} copy(bf16[864,3456]{1,0:T(8,128)(2,1)} %param.14) | data formatting | bytes 11943936 | tf_op args[5]
  64.0 3.7 shard_map.93.inverse
  67.7 2.1 copy-done.3
  73.5 2.5 collective-permute-start.10
  76.0 11.2 %collective-permute-done.8.refs_1_ = bf16[4,72,864]{2,1,0:T(8,128)(2,1)S(1)} collective-permute-done((bf16[4,72,864]{2,1,0:T(8,128)(2,1)S(1)}, bf16[4,72,864]{2,1,0:T(8,128)(2,1)S(1)}, u32[]{:S(2)}, u32[]{:S(2)}) %collective-permute-start.8) | collective-permute-done | bytes 497696 | tf_op jit(solution)/shard_map/ppermute | solution.py:35
  87.7 16.1 %collective-permute-done.9.refs_2_ = bf16[4,72,864]{2,1,0:T(8,128)(2,1)S(1)} collective-permute-done((bf16[4,72,864]{2,1,0:T(8,128)(2,1)S(1)}, bf16[4,72,864]{2,1,0:T(8,128)(2,1)S(1)}, u32[]{:S(2)}, u32[]{:S(2)}) %collective-permute-start.9) | collective-permute-done | bytes 497696 | tf_op jit(solution)/shard_map/ppermute | solution.py:35
  107.9 8.7 %shard_map.96 = (bf16[2,1840,128]{2,1,0:T(8,128)(2,1)S(1)}, bf16[2,1840,128]{2,1,0:T(8,128)(2,1)S(1)}, bf16[2,1728,128]{2,1,0:T(8,128)(2,1)}, bf16[2,1728,128]{2,1,0:T(8,128)(2,1)S(1)}) custom-call(s32[2]{0:T(128)S(1)} %pad_add_fusion.where, bf16[4,864,864]{2,1,0:T(8,128)(2,1)S(1)} %bitcast.171, bf16[4,72,864]{2,1,0:T(8,128)(2,1)S(1)} %get-tuple-element.111.refs_0_, ...), custom_call_target="tpu_custom_call" | custom-call | flops 3057647616 | bytes 10395648 | tf_op jit(solution)/shard_map/pallas_call | solution.py:328
  117.7 7.0 %collective-permute-done.24 = bf16[4,72,1280]{2,1,0:T(8,128)(2,1)S(1)} collective-permute-done((bf16[4,72,1280]{2,1,0:T(8,128)(2,1)S(1)}, bf16[4,72,1280]{2,1,0:T(8,128)(2,1)S(1)}, u32[]{:S(2)}, u32[]{:S(2)}) %collective-permute-start.24) | collective-permute-done | bytes 737312 | tf_op jit(solution)/shard_map/ppermute | solution.py:35
  124.7 14.1 %collective-permute-done.23 = bf16[4,72,1280]{2,1,0:T(8,128)(2,1)S(1)} collective-permute-done((bf16[4,72,1280]{2,1,0:T(8,128)(2,1)S(1)}, bf16[4,72,1280]{2,1,0:T(8,128)(2,1)S(1)}, u32[]{:S(2)}, u32[]{:S(2)}) %collective-permute-start.23) | collective-permute-done | bytes 737312 | tf_op jit(solution)/shard_map/ppermute | solution.py:35
  143.5 2.8 copy-done.1
  153.5 6.8 %shard_map.97 = (bf16[2,1728,128]{2,1,0:T(8,128)(2,1)S(1)}, bf16[2,1728,128]{2,1,0:T(8,128)(2,1)S(1)}, bf16[2,1728,128]{2,1,0:T(8,128)(2,1)}, bf16[2,1728,128]{2,1,0:T(8,128)(2,1)S(1)}) custom-call(s32[2]{0:T(128)S(1)} %pad_add_fusion.where, bf16[4,864,864]{2,1,0:T(8,128)(2,1)S(1)} %bitcast.172, bf16[4,72,864]{2,1,0:T(8,128)(2,1)S(1)} %get-tuple-element.111.refs_0_, ...), custom_call_target="tpu_custom_call" | custom-call | flops 3057647616 | bytes 10395648 | tf_op jit(solution)/shard_map/pallas_call | solution.py:328
  160.3 3.6 collective-permute-done.16
  171.4 5.9 %shard_map.99 = (bf16[2,1728,128]{2,1,0:T(8,128)(2,1)S(1)}, bf16[2,1728,128]{2,1,0:T(8,128)(2,1)S(1)}, bf16[2,1728,128]{2,1,0:T(8,128)(2,1)S(1)}, bf16[2,1728,128]{2,1,0:T(8,128)(2,1)S(1)}) custom-call(s32[2]{0:T(128)S(1)} %pad_add_fusion.where, bf16[4,864,864]{2,1,0:T(8,128)(2,1)S(1)} %bitcast.173, bf16[4,72,864]{2,1,0:T(8,128)(2,1)S(1)} %get-tuple-element.111.refs_0_, ...), custom_call_target="tpu_custom_call" | custom-call | flops 3057647616 | bytes 10395648 | tf_op jit(solution)/shard_map/pallas_call | solution.py:328
  177.3 1.9 collective-permute-done.19
  180.4 21.4 %shard_map.98 = (bf16[2,17,320,128]{3,2,1,0:T(8,128)(2,1)S(1)}, f32[16,8,256]{2,1,0:T(8,128)S(1)}) custom-call(s32[2]{0:T(128)S(1)} %pad_add_fusion.where, bf16[1,320,640]{2,1,0:T(8,128)(2,1)S(1)} %copy-done.51, bf16[1,320,640]{2,1,0:T(8,128)(2,1)} %collective-permute-done.4.refs_1_, bf16[1,320,640]{2,1,0:T(8,128)(2,1)} %collective-permute-done.5.refs_2_, ...), custom_call_target="tpu_custom_call" | custom-call | flops 3565158400 | bytes 10453000 | tf_op jit(solution)/shard_map/pallas_call | solution.py:67
  211.9 14.2 %collective-permute-start.29 = (bf16[1840,128]{1,0:T(8,128)(2,1)}, bf16[1840,128]{1,0:T(8,128)(2,1)S(1)}, u32[]{:S(2)}, u32[]{:S(2)}) collective-permute-start(bf16[1840,128]{1,0:T(8,128)(2,1)} %pad_maximum_fusion.8), channel_id=1, source_target_pairs={{0,8},{2,10},{4,12},{6,14},{8,0},{10,2},{12,4},{14,6},{16,24},{18,... | collective-permute-start | bytes 1413128 | tf_op jit(solution)/shard_map/ppermute | solution.py:35
  228.0 2.8 copy-done.2
  239.1 5.8 %shard_map.100 = (bf16[2,1728,128]{2,1,0:T(8,128)(2,1)S(1)}, bf16[2,1728,128]{2,1,0:T(8,128)(2,1)S(1)}, bf16[2,1728,128]{2,1,0:T(8,128)(2,1)S(1)}, bf16[2,1728,128]{2,1,0:T(8,128)(2,1)S(1)}) custom-call(s32[2]{0:T(128)S(1)} %pad_add_fusion.where, bf16[4,864,864]{2,1,0:T(8,128)(2,1)S(1)} %bitcast.174, bf16[4,72,864]{2,1,0:T(8,128)(2,1)S(1)} %copy-done.28, ...), custom_call_target="tpu_custom_call" | custom-call | flops 3057647616 | bytes 10395648 | tf_op jit(solution)/shard_map/pallas_call | solution.py:328
  247.8 6.9 %collective-permute-done.29 = bf16[1840,128]{1,0:T(8,128)(2,1)S(1)} collective-permute-done((bf16[1840,128]{1,0:T(8,128)(2,1)}, bf16[1840,128]{1,0:T(8,128)(2,1)S(1)}, u32[]{:S(2)}, u32[]{:S(2)}) %collective-permute-start.29) | collective-permute-done | bytes 471072 | tf_op jit(solution)/shard_map/ppermute | solution.py:35
  261.6 18.6 %collective-permute-done.33 = bf16[976,128]{1,0:T(8,128)(2,1)S(1)} collective-permute-done((bf16[976,128]{1,0:T(8,128)(2,1)S(1)}, bf16[976,128]{1,0:T(8,128)(2,1)S(1)}, u32[]{:S(2)}, u32[]{:S(2)}) %collective-permute-start.33) | collective-permute-done | bytes 249888 | tf_op jit(solution)/shard_map/ppermute | solution.py:35
  281.7 12.7 %collective-permute-done.32 = bf16[2,864,128]{2,1,0:T(8,128)(2,1)S(1)} collective-permute-done((bf16[2,864,128]{2,1,0:T(8,128)(2,1)S(1)}, bf16[2,864,128]{2,1,0:T(8,128)(2,1)S(1)}, u32[]{:S(2)}, u32[]{:S(2)}) %collective-permute-start.32) | collective-permute-done | bytes 442400 | tf_op jit(solution)/shard_map/ppermute | solution.py:35
  296.7 4.8 %collective-permute-done.37 = bf16[2,1728,128]{2,1,0:T(8,128)(2,1)} collective-permute-done((bf16[2,1728,128]{2,1,0:T(8,128)(2,1)S(1)}, bf16[2,1728,128]{2,1,0:T(8,128)(2,1)}, u32[]{:S(2)}, u32[]{:S(2)}) %collective-permute-start.37) | collective-permute-done | bytes 884768 | tf_op jit(solution)/shard_map/ppermute | solution.py:35
  302.9 2.9 collective-permute-start.39
  307.0 1.9 collective-permute-start.42
  309.2 10.6 %collective-permute-done.38 = bf16[1,864,128]{2,1,0:T(8,128)(2,1)S(1)} collective-permute-done((bf16[1,864,128]{2,1,0:T(8,128)(2,1)S(1)}, bf16[1,864,128]{2,1,0:T(8,128)(2,1)S(1)}, u32[]{:S(2)}, u32[]{:S(2)}) %collective-permute-start.38) | collective-permute-done | bytes 221216 | tf_op jit(solution)/shard_map/ppermute | solution.py:35
  319.8 4.4 collective-permute-done.39
  325.2 3.2 collective-permute-done.40
  329.9 2.0 collective-permute-start.46
  332.2 2.9 collective-permute-start.47
  335.2 23.0 %collective-permute-done.43 = bf16[16,128]{1,0:T(8,128)(2,1)S(1)} collective-permute-done((bf16[16,128]{1,0:T(8,128)(2,1)S(1)}, bf16[16,128]{1,0:T(8,128)(2,1)S(1)}, u32[]{:S(2)}, u32[]{:S(2)}) %collective-permute-start.43) | collective-permute-done | bytes 4128 | tf_op jit(solution)/shard_map/ppermute | solution.py:35
  361.2 2.6 collective-permute-done.48.refs_1_.refs_3_
  368.8 2.3 copy-done.4
  371.1 12.0 %shard_map.101 = f32[4,2,128]{2,1,0:T(2,128)S(1)} custom-call(s32[2]{0:T(128)S(1)} %pad_add_fusion.where, bf16[4,864,128]{2,1,0:T(8,128)(2,1)S(1)} %bitcast.176, f32[864,1280]{1,0:T(8,128)S(1)} %copy-done.4, f32[864,128]{1,0:T(8,128)S(1)} %pad_convert_fusion.query_b, f32[16,8,256]{2,1,0:T(8,128)S(1)} %get-tuple-element.174.info, ...), custom_call_target="tpu_custom_call" | custom-call | flops 18119393280 | bytes 8093696 | tf_op jit(solution)/shard_map/pallas_call | solution.py:391
  383.2 4.0 collective-permute-done.52
  387.9 3.4 collective-permute-start.55
  391.7 11.8 %shard_map.102 = f32[4,2,128]{2,1,0:T(2,128)S(1)} custom-call(s32[2]{0:T(128)S(1)} %pad_add_fusion.where, bf16[4,864,128]{2,1,0:T(8,128)(2,1)S(1)} %bitcast.178, f32[864,1280]{1,0:T(8,128)S(1)} %copy-done.4, f32[864,128]{1,0:T(8,128)S(1)} %pad_convert_fusion.query_b, f32[16,8,256]{2,1,0:T(8,128)S(1)} %get-tuple-element.174.info, ...), custom_call_target="tpu_custom_call" | custom-call | flops 18119393280 | bytes 8093696 | tf_op jit(solution)/shard_map/pallas_call | solution.py:391
  409.0 11.6 %shard_map.103 = f32[4,2,128]{2,1,0:T(2,128)S(1)} custom-call(s32[2]{0:T(128)S(1)} %pad_add_fusion.where, bf16[4,864,128]{2,1,0:T(8,128)(2,1)S(1)} %bitcast.179, f32[864,1280]{1,0:T(8,128)S(1)} %copy-done.4, f32[864,128]{1,0:T(8,128)S(1)} %pad_convert_fusion.query_b, f32[16,8,256]{2,1,0:T(8,128)S(1)} %get-tuple-element.174.info, ...), custom_call_target="tpu_custom_call" | custom-call | flops 18119393280 | bytes 8093696 | tf_op jit(solution)/shard_map/pallas_call | solution.py:391
  420.7 11.8 %shard_map.104 = f32[4,2,128]{2,1,0:T(2,128)S(1)} custom-call(s32[2]{0:T(128)S(1)} %pad_add_fusion.where, bf16[4,864,128]{2,1,0:T(8,128)(2,1)S(1)} %bitcast.177, f32[864,1280]{1,0:T(8,128)S(1)} %copy-done.4, f32[864,128]{1,0:T(8,128)S(1)} %pad_convert_fusion.query_b, f32[16,8,256]{2,1,0:T(8,128)S(1)} %get-tuple-element.174.info, ...), custom_call_target="tpu_custom_call" | custom-call | flops 18119393280 | bytes 8093696 | tf_op jit(solution)/shard_map/pallas_call | solution.py:391
  432.9 10.7 %all_to_all.5 = f32[16,2,16]{2,1,0:T(2,128)S(1)} all-to-all(f32[16,2,16]{2,1,0:T(2,128)S(1)} %multiply_reduce_fusion), channel_id=1, replica_groups=mesh['seq'=16,'eig'=2] {'seq'}, dimensions={0} | all-to-all | bytes 4096 | tf_op jit(solution)/shard_map/all_to_all | solution.py:619
  (344 shorter events, 100.2 us)
Async XLA Ops:
  6.5 295.0 %reduce-scatter.2.cloned.1.call-start = ((), (), s32[]{:S(2)}) async-start(), calls=%async_computation.2 | async-start | bytes 3481600 | tf_op jit(solution)/shard_map/reduce_scatter | solution.py:543
  16.7 15.9 %collective-permute-start = (bf16[1,320,864]{2,1,0:T(8,128)(2,1)S(1)}, bf16[1,320,864]{2,1,0:T(8,128)(2,1)S(1)}, u32[]{:S(2)}, u32[]{:S(2)}) collective-permute-start(bf16[1,320,864]{2,1,0:T(8,128)(2,1)S(1)} %get-tuple-element.98), channel_id=1, source_target_pairs={{0,2},{2,0},{4,6},{6,4},{8,10},{10,8},{12,14},{14,12},{16,18},{18,... | collective-permute-start | bytes 1658888 | tf_op jit(solution)/shard_map/ppermute | solution.py:35
  19.6 29.6 %collective-permute-start.3 = (bf16[72,4736]{1,0:T(8,128)(2,1)S(1)}, bf16[72,4736]{1,0:T(8,128)(2,1)S(1)}, u32[]{:S(2)}, u32[]{:S(2)}) collective-permute-start(bf16[72,4736]{1,0:T(8,128)(2,1)S(1)} %get-tuple-element.104), channel_id=1, source_target_pairs={{0,8},{2,10},{4,12},{6,14},{8,0},{10,2},{12,4},{14,6},{16,24},{18,... | collective-permute-start | bytes 2045960 | tf_op jit(solution)/shard_map/ppermute | solution.py:35
  21.2 30.1 %collective-permute-start.1 = (bf16[1,320,864]{2,1,0:T(8,128)(2,1)S(1)}, bf16[1,320,864]{2,1,0:T(8,128)(2,1)S(1)}, u32[]{:S(2)}, u32[]{:S(2)}) collective-permute-start(bf16[1,320,864]{2,1,0:T(8,128)(2,1)S(1)} %get-tuple-element.99), channel_id=1, source_target_pairs={{0,4},{2,6},{4,0},{6,2},{8,12},{10,14},{12,8},{14,10},{16,20},{18,... | collective-permute-start | bytes 1658888 | tf_op jit(solution)/shard_map/ppermute | solution.py:35
  22.7 48.6 %collective-permute-start.6 = (bf16[72,4736]{1,0:T(8,128)(2,1)}, bf16[72,4736]{1,0:T(8,128)(2,1)S(1)}, u32[]{:S(2)}, u32[]{:S(2)}) collective-permute-start(bf16[72,4736]{1,0:T(8,128)(2,1)} %get-tuple-element.109), channel_id=1, source_target_pairs={{0,16},{2,18},{4,20},{6,22},{8,24},{10,26},{12,28},{14,30},{16,0},... | collective-permute-start | bytes 2045960 | tf_op jit(solution)/shard_map/ppermute | solution.py:35
  25.3 46.0 %collective-permute-start.7 = (bf16[72,4736]{1,0:T(8,128)(2,1)}, bf16[72,4736]{1,0:T(8,128)(2,1)S(1)}, u32[]{:S(2)}, u32[]{:S(2)}) collective-permute-start(bf16[72,4736]{1,0:T(8,128)(2,1)} %get-tuple-element.110), channel_id=1, source_target_pairs={{0,24},{2,26},{4,28},{6,30},{8,16},{10,18},{12,20},{14,22},{16,8},... | collective-permute-start | bytes 2045960 | tf_op jit(solution)/shard_map/ppermute | solution.py:35
  33.4 28.5 %collective-permute-start.2 = (bf16[1,320,864]{2,1,0:T(8,128)(2,1)}, bf16[1,320,864]{2,1,0:T(8,128)(2,1)}, u32[]{:S(2)}, u32[]{:S(2)}) collective-permute-start(bf16[1,320,864]{2,1,0:T(8,128)(2,1)} %get-tuple-element.101), channel_id=1, source_target_pairs={{0,6},{2,4},{4,2},{6,0},{8,14},{10,12},{12,10},{14,8},{16,22},{18,... | collective-permute-start | bytes 1658888 | tf_op jit(solution)/shard_map/ppermute | solution.py:35
  49.2 20.5 %collective-permute-start.5 = (bf16[1,320,640]{2,1,0:T(8,128)(2,1)}, bf16[1,320,640]{2,1,0:T(8,128)(2,1)}, u32[]{:S(2)}, u32[]{:S(2)}) collective-permute-start(bf16[1,320,640]{2,1,0:T(8,128)(2,1)} %get-tuple-element.107), channel_id=1, source_target_pairs={{0,4},{2,6},{4,0},{6,2},{8,12},{10,14},{12,8},{14,10},{16,20},{18,... | collective-permute-start | bytes 1228808 | tf_op jit(solution)/shard_map/ppermute | solution.py:35
  52.1 17.6 %collective-permute-start.4 = (bf16[1,320,640]{2,1,0:T(8,128)(2,1)}, bf16[1,320,640]{2,1,0:T(8,128)(2,1)}, u32[]{:S(2)}, u32[]{:S(2)}) collective-permute-start(bf16[1,320,640]{2,1,0:T(8,128)(2,1)} %get-tuple-element.105), channel_id=1, source_target_pairs={{0,2},{2,0},{4,6},{6,4},{8,10},{10,8},{12,14},{14,12},{16,18},{18,... | collective-permute-start | bytes 1228808 | tf_op jit(solution)/shard_map/ppermute | solution.py:35
  73.0 30.8 %collective-permute-start.9 = (bf16[4,72,864]{2,1,0:T(8,128)(2,1)S(1)}, bf16[4,72,864]{2,1,0:T(8,128)(2,1)S(1)}, u32[]{:S(2)}, u32[]{:S(2)}) collective-permute-start(bf16[4,72,864]{2,1,0:T(8,128)(2,1)S(1)} %get-tuple-element.113), channel_id=1, source_target_pairs={{0,4},{2,6},{4,0},{6,2},{8,12},{10,14},{12,8},{14,10},{16,20},{18,... | collective-permute-start | bytes 1493000 | tf_op jit(solution)/shard_map/ppermute | solution.py:35
  73.5 30.4 %collective-permute-start.10 = (bf16[4,72,864]{2,1,0:T(8,128)(2,1)S(1)}, bf16[4,72,864]{2,1,0:T(8,128)(2,1)S(1)}, u32[]{:S(2)}, u32[]{:S(2)}) collective-permute-start(bf16[4,72,864]{2,1,0:T(8,128)(2,1)S(1)} %get-tuple-element.114), channel_id=1, source_target_pairs={{0,6},{2,4},{4,2},{6,0},{8,14},{10,12},{12,10},{14,8},{16,22},{18,... | collective-permute-start | bytes 1493000 | tf_op jit(solution)/shard_map/ppermute | solution.py:35
  76.0 29.1 %collective-permute-start.11 = (bf16[4,72,864]{2,1,0:T(8,128)(2,1)S(1)}, bf16[4,72,864]{2,1,0:T(8,128)(2,1)S(1)}, u32[]{:S(2)}, u32[]{:S(2)}) collective-permute-start(bf16[4,72,864]{2,1,0:T(8,128)(2,1)S(1)} %get-tuple-element.111.refs_0_), channel_id=1, source_target_pairs={{0,1},{1,0},{2,3},{3,2},{4,5},{5,4},{6,7},{7,6},{8,9},{9,8},{10,11... | collective-permute-start | bytes 1493000 | tf_op jit(solution)/shard_map/ppermute | solution.py:35
  87.2 19.2 %collective-permute-start.12 = (bf16[4,72,864]{2,1,0:T(8,128)(2,1)S(1)}, bf16[4,72,864]{2,1,0:T(8,128)(2,1)S(1)}, u32[]{:S(2)}, u32[]{:S(2)}) collective-permute-start(bf16[4,72,864]{2,1,0:T(8,128)(2,1)S(1)} %collective-permute-done.8.refs_1_), channel_id=1, source_target_pairs={{0,1},{1,0},{2,3},{3,2},{4,5},{5,4},{6,7},{7,6},{8,9},{9,8},{10,11... | collective-permute-start | bytes 1493000 | tf_op jit(solution)/shard_map/ppermute | solution.py:35
  87.2 17.2 %collective-permute-start.21 = (bf16[1,320,640]{2,1,0:T(8,128)(2,1)S(1)}, bf16[1,320,640]{2,1,0:T(8,128)(2,1)S(1)}, u32[]{:S(2)}, u32[]{:S(2)}) collective-permute-start(bf16[1,320,640]{2,1,0:T(8,128)(2,1)S(1)} %copy-done.55), channel_id=1, source_target_pairs={{0,6},{2,4},{4,2},{6,0},{8,14},{10,12},{12,10},{14,8},{16,22},{18,... | collective-permute-start | bytes 1228808 | tf_op jit(solution)/shard_map/ppermute | solution.py:35
  104.4 20.3 %collective-permute-start.24 = (bf16[4,72,1280]{2,1,0:T(8,128)(2,1)S(1)}, bf16[4,72,1280]{2,1,0:T(8,128)(2,1)S(1)}, u32[]{:S(2)}, u32[]{:S(2)}) collective-permute-start(bf16[4,72,1280]{2,1,0:T(8,128)(2,1)S(1)} %get-tuple-element.133), channel_id=1, source_target_pairs={{0,6},{2,4},{4,2},{6,0},{8,14},{10,12},{12,10},{14,8},{16,22},{18,... | collective-permute-start | bytes 2211848 | tf_op jit(solution)/shard_map/ppermute | solution.py:35
  105.1 33.7 %collective-permute-start.23 = (bf16[4,72,1280]{2,1,0:T(8,128)(2,1)S(1)}, bf16[4,72,1280]{2,1,0:T(8,128)(2,1)S(1)}, u32[]{:S(2)}, u32[]{:S(2)}) collective-permute-start(bf16[4,72,1280]{2,1,0:T(8,128)(2,1)S(1)} %get-tuple-element.133), channel_id=1, source_target_pairs={{0,4},{2,6},{4,0},{6,2},{8,12},{10,14},{12,8},{14,10},{16,20},{18,... | collective-permute-start | bytes 2211848 | tf_op jit(solution)/shard_map/ppermute | solution.py:35
  106.4 32.4 %collective-permute-start.22 = (bf16[4,72,1280]{2,1,0:T(8,128)(2,1)S(1)}, bf16[4,72,1280]{2,1,0:T(8,128)(2,1)S(1)}, u32[]{:S(2)}, u32[]{:S(2)}) collective-permute-start(bf16[4,72,1280]{2,1,0:T(8,128)(2,1)S(1)} %get-tuple-element.133), channel_id=1, source_target_pairs={{0,2},{2,0},{4,6},{6,4},{8,10},{10,8},{12,14},{14,12},{16,18},{18,... | collective-permute-start | bytes 2211848 | tf_op jit(solution)/shard_map/ppermute | solution.py:35
  141.5 38.8 %collective-permute-start.25 = (bf16[16,72,1280]{2,1,0:T(8,128)(2,1)}, bf16[16,72,1280]{2,1,0:T(8,128)(2,1)}, u32[]{:S(2)}, u32[]{:S(2)}) collective-permute-start(bf16[16,72,1280]{2,1,0:T(8,128)(2,1)} %constant_dynamic-update-slice_fusion.refs_4_), channel_id=1, source_target_pairs={{0,1},{1,0},{2,3},{3,2},{4,5},{5,4},{6,7},{7,6},{8,9},{9,8},{10,11... | collective-permute-start | bytes 8847368 | tf_op jit(solution)/shard_map/ppermute | solution.py:35
  141.6 22.4 %collective-permute-start.16 = (bf16[2,1728,128]{2,1,0:T(8,128)(2,1)}, bf16[2,1728,128]{2,1,0:T(8,128)(2,1)}, u32[]{:S(2)}, u32[]{:S(2)}) collective-permute-start(bf16[2,1728,128]{2,1,0:T(8,128)(2,1)} %get-tuple-element.115), channel_id=1, source_target_pairs={{0,4},{2,6},{4,0},{6,2},{8,12},{10,14},{12,8},{14,10},{16,20},{18,... | collective-permute-start | bytes 2654216 | tf_op jit(solution)/shard_map/ppermute | solution.py:35
  143.0 23.1 %collective-permute-start.15 = (bf16[2,1840,128]{2,1,0:T(8,128)(2,1)S(1)}, bf16[2,1840,128]{2,1,0:T(8,128)(2,1)}, u32[]{:S(2)}, u32[]{:S(2)}) collective-permute-start(bf16[2,1840,128]{2,1,0:T(8,128)(2,1)S(1)} %get-tuple-element.119), channel_id=1, source_target_pairs={{0,2},{2,0},{4,6},{6,4},{8,10},{10,8},{12,14},{14,12},{16,18},{18,... | collective-permute-start | bytes 2826248 | tf_op jit(solution)/shard_map/ppermute | solution.py:35
  167.7 34.7 %collective-permute-start.18 = (bf16[1840,128]{1,0:T(8,128)(2,1)S(1)}, bf16[1840,128]{1,0:T(8,128)(2,1)S(1)}, u32[]{:S(2)}, u32[]{:S(2)}) collective-permute-start(bf16[1840,128]{1,0:T(8,128)(2,1)S(1)} %fusion.12), channel_id=1, source_target_pairs={{0,4},{2,6},{4,0},{6,2},{8,12},{10,14},{12,8},{14,10},{16,20},{18,... | collective-permute-start | bytes 1413128 | tf_op jit(solution)/shard_map/ppermute | solution.py:35
  169.2 39.3 %collective-permute-start.20 = (bf16[2,1728,128]{2,1,0:T(8,128)(2,1)}, bf16[2,1728,128]{2,1,0:T(8,128)(2,1)}, u32[]{:S(2)}, u32[]{:S(2)}) collective-permute-start(bf16[2,1728,128]{2,1,0:T(8,128)(2,1)} %get-tuple-element.126), channel_id=1, source_target_pairs={{0,4},{2,6},{4,0},{6,2},{8,12},{10,14},{12,8},{14,10},{16,20},{18,... | collective-permute-start | bytes 2654216 | tf_op jit(solution)/shard_map/ppermute | solution.py:35
  169.8 35.7 %collective-permute-start.17 = (bf16[2,1728,128]{2,1,0:T(8,128)(2,1)S(1)}, bf16[2,1728,128]{2,1,0:T(8,128)(2,1)S(1)}, u32[]{:S(2)}, u32[]{:S(2)}) collective-permute-start(bf16[2,1728,128]{2,1,0:T(8,128)(2,1)S(1)} %get-tuple-element.121), channel_id=1, source_target_pairs={{0,2},{2,0},{4,6},{6,4},{8,10},{10,8},{12,14},{14,12},{16,18},{18,... | collective-permute-start | bytes 2654216 | tf_op jit(solution)/shard_map/ppermute | solution.py:35
  208.5 149.7 %all-gather.2.cloned.1.call-start = ((), (), s32[]{:S(2)}) async-start(), calls=%async_computation.3 | async-start | bytes 3481600 | tf_op jit(solution)/shard_map/all_gather | solution.py:586
  208.6 36.4 %collective-permute-start.27 = (bf16[1728,128]{1,0:T(8,128)(2,1)S(1)}, bf16[1728,128]{1,0:T(8,128)(2,1)S(1)}, u32[]{:S(2)}, u32[]{:S(2)}) collective-permute-start(bf16[1728,128]{1,0:T(8,128)(2,1)S(1)} %fusion.13), channel_id=1, source_target_pairs={{0,4},{2,6},{4,0},{6,2},{8,12},{10,14},{12,8},{14,10},{16,20},{18,... | collective-permute-start | bytes 1327112 | tf_op jit(solution)/shard_map/ppermute | solution.py:35
  210.9 34.4 %collective-permute-start.28 = (bf16[1728,128]{1,0:T(8,128)(2,1)S(1)}, bf16[1728,128]{1,0:T(8,128)(2,1)S(1)}, u32[]{:S(2)}, u32[]{:S(2)}) collective-permute-start(bf16[1728,128]{1,0:T(8,128)(2,1)S(1)} %fusion.15), channel_id=1, source_target_pairs={{0,2},{2,0},{4,6},{6,4},{8,10},{10,8},{12,14},{14,12},{16,18},{18,... | collective-permute-start | bytes 1327112 | tf_op jit(solution)/shard_map/ppermute | solution.py:35
  211.9 42.8 %collective-permute-start.29 = (bf16[1840,128]{1,0:T(8,128)(2,1)}, bf16[1840,128]{1,0:T(8,128)(2,1)S(1)}, u32[]{:S(2)}, u32[]{:S(2)}) collective-permute-start(bf16[1840,128]{1,0:T(8,128)(2,1)} %pad_maximum_fusion.8), channel_id=1, source_target_pairs={{0,8},{2,10},{4,12},{6,14},{8,0},{10,2},{12,4},{14,6},{16,24},{18,... | collective-permute-start | bytes 1413128 | tf_op jit(solution)/shard_map/ppermute | solution.py:35
  226.1 29.5 %collective-permute-start.31 = (bf16[2,1728,128]{2,1,0:T(8,128)(2,1)}, bf16[2,1728,128]{2,1,0:T(8,128)(2,1)S(1)}, u32[]{:S(2)}, u32[]{:S(2)}) collective-permute-start(bf16[2,1728,128]{2,1,0:T(8,128)(2,1)} %copy-done.26), channel_id=1, source_target_pairs={{0,4},{2,6},{4,0},{6,2},{8,12},{10,14},{12,8},{14,10},{16,20},{18,... | collective-permute-start | bytes 2654216 | tf_op jit(solution)/shard_map/ppermute | solution.py:35
  227.1 28.5 %collective-permute-start.30 = (bf16[2,1728,128]{2,1,0:T(8,128)(2,1)}, bf16[2,1728,128]{2,1,0:T(8,128)(2,1)S(1)}, u32[]{:S(2)}, u32[]{:S(2)}) collective-permute-start(bf16[2,1728,128]{2,1,0:T(8,128)(2,1)} %copy-done.25), channel_id=1, source_target_pairs={{0,2},{2,0},{4,6},{6,4},{8,10},{10,8},{12,14},{14,12},{16,18},{18,... | collective-permute-start | bytes 2654216 | tf_op jit(solution)/shard_map/ppermute | solution.py:35
  255.7 24.5 %collective-permute-start.33 = (bf16[976,128]{1,0:T(8,128)(2,1)S(1)}, bf16[976,128]{1,0:T(8,128)(2,1)S(1)}, u32[]{:S(2)}, u32[]{:S(2)}) collective-permute-start(bf16[976,128]{1,0:T(8,128)(2,1)S(1)} %pad_maximum_fusion.13), channel_id=1, source_target_pairs={{0,16},{2,18},{4,20},{6,22},{8,24},{10,26},{12,28},{14,30},{16,0},... | collective-permute-start | bytes 749576 | tf_op jit(solution)/shard_map/ppermute | solution.py:35
  257.2 37.2 %collective-permute-start.32 = (bf16[2,864,128]{2,1,0:T(8,128)(2,1)S(1)}, bf16[2,864,128]{2,1,0:T(8,128)(2,1)S(1)}, u32[]{:S(2)}, u32[]{:S(2)}) collective-permute-start(bf16[2,864,128]{2,1,0:T(8,128)(2,1)S(1)} %dynamic-slice_bitcast_fusion.5), channel_id=1, source_target_pairs={{0,8},{2,10},{4,12},{6,14},{8,0},{10,2},{12,4},{14,6},{16,24},{18,... | collective-permute-start | bytes 1327112 | tf_op jit(solution)/shard_map/ppermute | solution.py:35
  259.2 35.3 %collective-permute-start.34 = (bf16[1728,128]{1,0:T(8,128)(2,1)S(1)}, bf16[1728,128]{1,0:T(8,128)(2,1)S(1)}, u32[]{:S(2)}, u32[]{:S(2)}) collective-permute-start(bf16[1728,128]{1,0:T(8,128)(2,1)S(1)} %fusion.16), channel_id=1, source_target_pairs={{0,4},{2,6},{4,0},{6,2},{8,12},{10,14},{12,8},{14,10},{16,20},{18,... | collective-permute-start | bytes 1327112 | tf_op jit(solution)/shard_map/ppermute | solution.py:35
  259.5 36.0 %collective-permute-start.35 = (bf16[1728,128]{1,0:T(8,128)(2,1)S(1)}, bf16[1728,128]{1,0:T(8,128)(2,1)S(1)}, u32[]{:S(2)}, u32[]{:S(2)}) collective-permute-start(bf16[1728,128]{1,0:T(8,128)(2,1)S(1)} %fusion.17), channel_id=1, source_target_pairs={{0,2},{2,0},{4,6},{6,4},{8,10},{10,8},{12,14},{14,12},{16,18},{18,... | collective-permute-start | bytes 1327112 | tf_op jit(solution)/shard_map/ppermute | solution.py:35
  259.9 35.8 %collective-permute-start.36 = (bf16[2,1728,128]{2,1,0:T(8,128)(2,1)S(1)}, bf16[2,1728,128]{2,1,0:T(8,128)(2,1)S(1)}, u32[]{:S(2)}, u32[]{:S(2)}) collective-permute-start(bf16[2,1728,128]{2,1,0:T(8,128)(2,1)S(1)} %get-tuple-element.156), channel_id=1, source_target_pairs={{0,2},{2,0},{4,6},{6,4},{8,10},{10,8},{12,14},{14,12},{16,18},{18,... | collective-permute-start | bytes 2654216 | tf_op jit(solution)/shard_map/ppermute | solution.py:35
  280.2 21.3 %collective-permute-start.37 = (bf16[2,1728,128]{2,1,0:T(8,128)(2,1)S(1)}, bf16[2,1728,128]{2,1,0:T(8,128)(2,1)}, u32[]{:S(2)}, u32[]{:S(2)}) collective-permute-start(bf16[2,1728,128]{2,1,0:T(8,128)(2,1)S(1)} %get-tuple-element.157), channel_id=1, source_target_pairs={{0,4},{2,6},{4,0},{6,2},{8,12},{10,14},{12,8},{14,10},{16,20},{18,... | collective-permute-start | bytes 2654216 | tf_op jit(solution)/shard_map/ppermute | solution.py:35
  302.8 16.9 %collective-permute-start.38 = (bf16[1,864,128]{2,1,0:T(8,128)(2,1)S(1)}, bf16[1,864,128]{2,1,0:T(8,128)(2,1)S(1)}, u32[]{:S(2)}, u32[]{:S(2)}) collective-permute-start(bf16[1,864,128]{2,1,0:T(8,128)(2,1)S(1)} %constant_dynamic-slice_fusion.2), channel_id=1, source_target_pairs={{0,16},{2,18},{4,20},{6,22},{8,24},{10,26},{12,28},{14,30},{16,0},... | collective-permute-start | bytes 663560 | tf_op jit(solution)/shard_map/ppermute | solution.py:35
  302.9 21.3 %collective-permute-start.39 = (bf16[864,128]{1,0:T(8,128)(2,1)S(1)}, bf16[864,128]{1,0:T(8,128)(2,1)S(1)}, u32[]{:S(2)}, u32[]{:S(2)}) collective-permute-start(bf16[864,128]{1,0:T(8,128)(2,1)S(1)} %fusion.20), channel_id=1, source_target_pairs={{0,16},{2,18},{4,20},{6,22},{8,24},{10,26},{12,28},{14,30},{16,0},... | collective-permute-start | bytes 663560 | tf_op jit(solution)/shard_map/ppermute | solution.py:35
  307.0 18.2 %collective-permute-start.42 = (bf16[1728,128]{1,0:T(8,128)(2,1)S(1)}, bf16[1728,128]{1,0:T(8,128)(2,1)S(1)}, u32[]{:S(2)}, u32[]{:S(2)}) collective-permute-start(bf16[1728,128]{1,0:T(8,128)(2,1)S(1)} %fusion.19), channel_id=1, source_target_pairs={{0,2},{2,0},{4,6},{6,4},{8,10},{10,8},{12,14},{14,12},{16,18},{18,... | collective-permute-start | bytes 1327112 | tf_op jit(solution)/shard_map/ppermute | solution.py:35
  308.9 19.4 %collective-permute-start.40 = (bf16[2,864,128]{2,1,0:T(8,128)(2,1)S(1)}, bf16[2,864,128]{2,1,0:T(8,128)(2,1)S(1)}, u32[]{:S(2)}, u32[]{:S(2)}) collective-permute-start(bf16[2,864,128]{2,1,0:T(8,128)(2,1)S(1)} %dynamic-slice_bitcast_fusion.4), channel_id=1, source_target_pairs={{0,8},{2,10},{4,12},{6,14},{8,0},{10,2},{12,4},{14,6},{16,24},{18,... | collective-permute-start | bytes 1327112 | tf_op jit(solution)/shard_map/ppermute | solution.py:35
  308.9 19.4 %collective-permute-start.41 = (bf16[1728,128]{1,0:T(8,128)(2,1)S(1)}, bf16[1728,128]{1,0:T(8,128)(2,1)S(1)}, u32[]{:S(2)}, u32[]{:S(2)}) collective-permute-start(bf16[1728,128]{1,0:T(8,128)(2,1)S(1)} %fusion.18), channel_id=1, source_target_pairs={{0,4},{2,6},{4,0},{6,2},{8,12},{10,14},{12,8},{14,10},{16,20},{18,... | collective-permute-start | bytes 1327112 | tf_op jit(solution)/shard_map/ppermute | solution.py:35
  329.8 28.4 %collective-permute-start.44 = (bf16[1712,128]{1,0:T(8,128)(2,1)S(1)}, bf16[1712,128]{1,0:T(8,128)(2,1)}, u32[]{:S(2)}, u32[]{:S(2)}) collective-permute-start(bf16[1712,128]{1,0:T(8,128)(2,1)S(1)} %pad_maximum_fusion.12), channel_id=1, source_target_pairs={{0,8},{2,10},{4,12},{6,14},{8,0},{10,2},{12,4},{14,6},{16,24},{18,... | collective-permute-start | bytes 1314824 | tf_op jit(solution)/shard_map/ppermute | solution.py:35
  329.9 28.3 %collective-permute-start.46 = (bf16[2,864,128]{2,1,0:T(8,128)(2,1)S(1)}, bf16[2,864,128]{2,1,0:T(8,128)(2,1)S(1)}, u32[]{:S(2)}, u32[]{:S(2)}) collective-permute-start(bf16[2,864,128]{2,1,0:T(8,128)(2,1)S(1)} %dynamic-slice_bitcast_fusion.3), channel_id=1, source_target_pairs={{0,8},{2,10},{4,12},{6,14},{8,0},{10,2},{12,4},{14,6},{16,24},{18,... | collective-permute-start | bytes 1327112 | tf_op jit(solution)/shard_map/ppermute | solution.py:35
  332.1 26.1 %collective-permute-start.45 = (bf16[864,128]{1,0:T(8,128)(2,1)S(1)}, bf16[864,128]{1,0:T(8,128)(2,1)S(1)}, u32[]{:S(2)}, u32[]{:S(2)}) collective-permute-start(bf16[864,128]{1,0:T(8,128)(2,1)S(1)} %bitcast.191), channel_id=1, source_target_pairs={{0,16},{2,18},{4,20},{6,22},{8,24},{10,26},{12,28},{14,30},{16,0},... | collective-permute-start | bytes 663560 | tf_op jit(solution)/shard_map/ppermute | solution.py:35
  332.2 26.0 %collective-permute-start.47 = (bf16[1,864,128]{2,1,0:T(8,128)(2,1)S(1)}, bf16[1,864,128]{2,1,0:T(8,128)(2,1)S(1)}, u32[]{:S(2)}, u32[]{:S(2)}) collective-permute-start(bf16[1,864,128]{2,1,0:T(8,128)(2,1)S(1)} %constant_dynamic-slice_fusion.1), channel_id=1, source_target_pairs={{0,16},{2,18},{4,20},{6,22},{8,24},{10,26},{12,28},{14,30},{16,0},... | collective-permute-start | bytes 663560 | tf_op jit(solution)/shard_map/ppermute | solution.py:35
  335.1 23.1 %collective-permute-start.43 = (bf16[16,128]{1,0:T(8,128)(2,1)S(1)}, bf16[16,128]{1,0:T(8,128)(2,1)S(1)}, u32[]{:S(2)}, u32[]{:S(2)}) collective-permute-start(bf16[16,128]{1,0:T(8,128)(2,1)S(1)} %slice_bitcast_fusion.2), channel_id=1, source_target_pairs={{0,8},{2,10},{4,12},{6,14},{8,0},{10,2},{12,4},{14,6},{16,24},{18,... | collective-permute-start | bytes 12296 | tf_op jit(solution)/shard_map/ppermute | solution.py:35
  364.8 22.6 %collective-permute-start.51 = (bf16[864,128]{1,0:T(8,128)(2,1)S(1)}, bf16[864,128]{1,0:T(8,128)(2,1)S(1)}, u32[]{:S(2)}, u32[]{:S(2)}) collective-permute-start(bf16[864,128]{1,0:T(8,128)(2,1)S(1)} %bitcast.195), channel_id=1, source_target_pairs={{0,16},{2,18},{4,20},{6,22},{8,24},{10,26},{12,28},{14,30},{16,0},... | collective-permute-start | bytes 663560 | tf_op jit(solution)/shard_map/ppermute | solution.py:35
  366.0 21.2 %collective-permute-start.52 = (bf16[1,864,128]{2,1,0:T(8,128)(2,1)S(1)}, bf16[1,864,128]{2,1,0:T(8,128)(2,1)S(1)}, u32[]{:S(2)}, u32[]{:S(2)}) collective-permute-start(bf16[1,864,128]{2,1,0:T(8,128)(2,1)S(1)} %constant_dynamic-slice_fusion), channel_id=1, source_target_pairs={{0,16},{2,18},{4,20},{6,22},{8,24},{10,26},{12,28},{14,30},{16,0},... | collective-permute-start | bytes 663560 | tf_op jit(solution)/shard_map/ppermute | solution.py:35
  367.8 20.1 %collective-permute-start.50 = (bf16[1712,128]{1,0:T(8,128)(2,1)S(1)}, bf16[1712,128]{1,0:T(8,128)(2,1)S(1)}, u32[]{:S(2)}, u32[]{:S(2)}) collective-permute-start(bf16[1712,128]{1,0:T(8,128)(2,1)S(1)} %pad_maximum_fusion.11), channel_id=1, source_target_pairs={{0,8},{2,10},{4,12},{6,14},{8,0},{10,2},{12,4},{14,6},{16,24},{18,... | collective-permute-start | bytes 1314824 | tf_op jit(solution)/shard_map/ppermute | solution.py:35
  (84 other events, 731.9 us)
Sparse Core Ops, SparseCore 0:
  208.6 89.9 reduce-scatter.1
  301.7 45.1 all-gather.1
